TPU v7x, 256 devices: a whole 4x4x8 slice. The times are simulated.
256 devices in a mesh: blk: 64 (over x, y_hi, z), rep: 4 (over y_lo, core).
Axes of the slice: x: 4, y: 4 (y_hi: 2, y_lo: 2; y = y_hi * 2 + y_lo), z: 8, core: 2. Of those that a mesh axis runs over, the one named last changes fastest.
Arguments:
- features: bfloat16 [32768, 512], P('blk', 'rep'), may hold values from -6 to 6
- row_target: int32 [32768], P('blk'), may hold values from 0 to 32767, as said below
- tile_values: bfloat16 [64, 64, 4, 128, 128], P('blk'), may hold values from -0.25 to 0.25
- tile_rows: int32 [64, 64, 4], P('blk'), may hold values from 0 to 3, as said below
- tile_cols: int32 [64, 64, 4], P('blk'), may hold values from 0 to 3, as said below
- tile_counts: int32 [64, 64], P('blk'), may hold values from 0 to 4, as said below
- weight: bfloat16 [512, 512], P('rep'), may hold values from -0.25 to 0.25
- layer_bias: float32 [512], replicated, may hold values from -3 to 3
- out_grad: bfloat16 [32768, 512], P('blk'), may hold values from -0.75 to 0.75
Outputs:
- output: bfloat16 [32768, 512], P(('blk', 'rep'))
- weight_grad: float32 [512, 512], P('rep')
- bias_grad: float32 [512], replicated
- feature_grad: bfloat16 [32768, 512], P('blk', 'rep')
Inputs may be any that keep to these rules, and one draw needn't show every extreme that they name: `row_target`: a permutation of the 32768 rows; the rows of one loader block of 512 rows bound for one partition number at most 16, and this many in every draw. `tile_rows`: within one pair of partitions the live slots name distinct tile positions. `tile_cols`: within one pair of partitions the live slots name distinct tile positions. `tile_counts`: every pair of a partition with itself has all 4 slots live; each row partition has live slots with exactly 6 other partitions, and none with the rest.
All inputs are finite; a program needn't handle non-finite values.
Results may differ from a plain program's by a relative error of at most 0.0061.
Values may be sent and summed in bfloat16 or wider, within the bound.
A program may use at most 128 MiB of HBM per device.

v0:
```python
import jax
import jax.numpy as jnp
from jax import lax
from jax.sharding import PartitionSpec as P


def per_device(
    features,
    row_target,
    tile_values,
    tile_rows,
    tile_cols,
    tile_counts,
    weight,
    layer_bias,
    out_grad,
):
    block_count = lax.axis_size("blk")
    member_count = lax.axis_size("rep")
    row_count = features.shape[0]
    column_share = features.shape[1]
    slot_count = tile_values.shape[2]
    tile_size = tile_values.shape[3]
    row_tiles = row_count // tile_size
    bucket = 2 * row_count // block_count
    target = row_target // row_count
    landing_spot = row_target % row_count
    hits = (target[:, None] == jnp.arange(block_count, dtype=jnp.int32)[None, :]).astype(jnp.int32)
    ranked = jnp.sum(hits * jnp.cumsum(hits, axis=0), axis=1) - 1
    flat_slot = target * bucket + ranked
    send_rows = (
        jnp.zeros((block_count * bucket, column_share), jnp.bfloat16).at[flat_slot].set(features)
    )
    send_rows = send_rows.reshape(block_count, bucket, column_share)
    send_where = jnp.full((block_count * bucket,), -1, jnp.int32).at[flat_slot].set(landing_spot)
    send_where = send_where.reshape(block_count, bucket)
    got_rows, got_where = (
        lax.all_to_all(send_rows, "blk", split_axis=0, concat_axis=0, tiled=True),
        lax.all_to_all(send_where, "blk", split_axis=0, concat_axis=0, tiled=True),
    )
    got_where = got_where.reshape(-1)
    landing = jnp.where(got_where >= 0, got_where, row_count)
    regrouped = (
        jnp.zeros((row_count, column_share), jnp.bfloat16)
        .at[landing]
        .set(got_rows.reshape(-1, column_share), mode="drop")
    )
    values = tile_values[0]
    row_ids = tile_rows[0]
    col_ids = tile_cols[0]
    live_counts = tile_counts[0]
    slot_range = jnp.arange(slot_count, dtype=jnp.int32)

    def place_tiles(product, index, live, total):
        where_to = jnp.where(live, index, total).reshape(-1)
        flat = product.reshape(-1, tile_size, column_share)
        placed = (
            jnp.zeros((total, tile_size, column_share), jnp.float32)
            .at[where_to]
            .add(flat, mode="drop")
        )
        return placed.reshape(total * tile_size, column_share)

    piece = lax.all_gather(regrouped, "blk", axis=0, tiled=True)
    span_count = piece.shape[0] // row_count
    sub_values = values
    sub_rows = row_ids
    sub_cols = col_ids
    sub_live = live_counts
    live = slot_range[None, :] < sub_live[:, None]
    local = jnp.arange(span_count, dtype=jnp.int32)[:, None] * row_tiles + sub_cols
    inputs = piece.reshape(span_count * row_tiles, tile_size, column_share)[local]
    product = jnp.einsum("qsij,qsjf->qsif", sub_values, inputs, preferred_element_type=jnp.float32)
    mixed = place_tiles(product, sub_rows, live, row_tiles).astype(jnp.bfloat16)
    share = row_count // member_count
    member = lax.axis_index("rep")
    partial_pre = jnp.dot(mixed, weight, preferred_element_type=jnp.float32)
    pre = lax.psum(partial_pre, "rep") + layer_bias
    sigma = jax.nn.sigmoid(pre)
    own_pre = lax.dynamic_slice_in_dim(pre, member * share, share, 0)
    own_sigma = lax.dynamic_slice_in_dim(sigma, member * share, share, 0)
    output = (own_pre * own_sigma).astype(jnp.bfloat16)
    pre_grad = (out_grad.astype(jnp.float32) * sigma * (1.0 + pre * (1.0 - sigma))).astype(
        jnp.bfloat16
    )
    weight_part = lax.dot_general(
        mixed, pre_grad, (((0,), (0,)), ((), ())), preferred_element_type=jnp.float32
    )
    bias_part = jnp.sum(pre_grad.astype(jnp.float32), axis=0)
    weight_grad, bias_grad = lax.psum((weight_part, bias_part), "blk")
    mixed_grad = lax.dot_general(
        pre_grad, weight, (((1,), (1,)), ((), ())), preferred_element_type=jnp.float32
    ).astype(jnp.bfloat16)
    grad_tiles = mixed_grad.reshape(row_tiles, tile_size, column_share)
    span_count = lax.axis_size("blk") * row_count // row_count
    sub_values = values
    sub_rows = row_ids
    sub_cols = col_ids
    sub_live = live_counts
    live = slot_range[None, :] < sub_live[:, None]
    inputs = grad_tiles[sub_rows]
    product = jnp.einsum("qsij,qsif->qsjf", sub_values, inputs, preferred_element_type=jnp.float32)
    column = jnp.arange(span_count, dtype=jnp.int32)[:, None] * row_tiles + sub_cols
    feature_grad = lax.psum_scatter(
        place_tiles(product, column, live, span_count * row_tiles),
        "blk",
        scatter_dimension=0,
        tiled=True,
    ).astype(jnp.bfloat16)
    return (output, weight_grad, bias_grad, feature_grad)


def solution(mesh):
    in_specs = (
        P("blk", "rep"),
        P("blk"),
        P("blk", None, None, None, None),
        P("blk", None, None),
        P("blk", None, None),
        P("blk", None),
        P("rep", None),
        P(),
        P("blk", None),
    )
    out_specs = (P(("blk", "rep"), None), P("rep", None), P(), P("blk", "rep"))
    return jax.shard_map(
        per_device, mesh=mesh, in_specs=in_specs, out_specs=out_specs, check_vma=False
    )
```

profile of v0, /device:TPU:1, one launch (start us, length us, event | category | flops | bytes accessed | tf_op | source)
XLA Modules:
  0.0 1436.4 jit_solution(16725088751572145060)
XLA Ops:
  9.5 2.4 scatter_custom_fusion
  12.7 15.1 %all-to-all-start = ((s32[64,1,16]{2,1,0:T(1,128)}), s32[64,1,16]{2,1,0:T(1,128)S(1)}, u32[]{:S(2)}, u32[]{:S(2)}) async-start(s32[64,1,16]{2,1,0:T(1,128)} %bitcast.4), calls=%async_computation | async-start | bytes 65536 | tf_op jit(solution)/shard_map/all_to_all | solution.py:39
  27.8 2.8 scatter_custom_fusion.1
  30.6 7.9 all-to-all-done
  38.5 4.6 all-to-all-start.1
  44.5 11.1 all-to-all-done.1
  55.7 3.8 scatter_custom_fusion.2
  63.4 136.8 %all-gather.2.cloned.1.call-done = bf16[32768,128]{1,0:T(8,128)(2,1)} async-done(((bf16[512,128]{1,0:T(8,128)(2,1)}), bf16[32768,128]{1,0:T(8,128)(2,1)}) %all-gather.2.cloned.1.call-update) | async-done | bytes 8388624 | tf_op jit(solution)/shard_map/all_gather | solution.py:64
  200.2 12.0 gather_fusion
  212.2 12.8 fusion.2
  225.0 17.5 %copy.28 = f32[256,128,128]{2,1,0:T(8,128)} copy(f32[256,128,128]{1,2,0:T(8,128)} %bitcast.65) | data formatting | bytes 33554432 | tf_op jit(solution)/shard_map/reshape | solution.py:56
  242.5 33.1 %scatter_fusion = f32[4,128,128]{2,1,0:T(8,128)S(1)} fusion(f32[4,128,128]{2,1,0:T(8,128)S(1)} %broadcast_in_dim.42, s32[256]{0:T(256)S(1)} %bitcast.74, f32[256,128,128]{2,1,0:T(8,128)} %copy.28), kind=kCustom, calls=%fused_computation.5 | custom fusion | flops 4194304 | bytes 50332672 | tf_op jit(solution)/shard_map/scatter-add | solution.py:60
  277.5 45.7 %all-reduce.3.cloned.1.call-done = f32[512,512]{1,0:T(8,128)} async-done(((f32[512,512]{1,0:T(8,128)}), f32[512,512]{1,0:T(8,128)}) %all-reduce.3.cloned.1.call-update) | async-done | bytes 1048592 | tf_op jit(solution)/shard_map/psum | solution.py:78
  323.2 1.7 convert_reduce_fusion
  325.2 8.6 gather_fusion.1
  333.7 14.4 %fusion = f32[64,4,128,128]{3,2,1,0:T(8,128)} fusion(bf16[64,4,128,128]{3,2,1,0:T(8,128)(2,1)} %bitcast.66, bf16[1,64,4,128,128]{4,3,2,1,0:T(8,128)(2,1)} %param.11), kind=kOutput, calls=%fused_computation.7 | convolution fusion | flops 1073741824 | bytes 33554432 | tf_op jit(solution)/shard_map/qsij,qsif->qsjf/dot_general | solution.py:102
  348.1 17.5 %copy.32 = f32[256,128,128]{2,1,0:T(8,128)} copy(f32[256,128,128]{1,2,0:T(8,128)} %bitcast.64) | data formatting | bytes 33554432 | tf_op jit(solution)/shard_map/reshape | solution.py:56
  365.6 7.8 broadcast_in_dim.49
  373.4 48.6 %scatter_fusion.1 = f32[256,128,128]{2,1,0:T(8,128)} fusion(f32[256,128,128]{2,1,0:T(8,128)} %broadcast_in_dim.49, s32[256]{0:T(256)S(1)} %bitcast.73, f32[256,128,128]{2,1,0:T(8,128)} %copy.32), kind=kCustom, calls=%fused_computation.6 | custom fusion | flops 4194304 | bytes 50332672 | tf_op jit(solution)/shard_map/scatter-add | solution.py:60
  422.1 163.8 %psum.23 = f32[512]{0:T(512)} all-reduce(f32[512]{0:T(512)S(1)} %get-tuple-element.4), channel_id=1, replica_groups=mesh['blk'=64,'rep'=4] {'blk'}, use_global_device_ids=true, to_apply=%region_10.11 | all-reduce | flops 512 | bytes 4096 | tf_op jit(solution)/shard_map/psum | solution.py:90
  587.9 187.4 %reduce-scatter.2.cloned.1.call-done = f32[512,128]{1,0:T(8,128)} async-done(((f32[32768,128]{1,0:T(8,128)}), f32[512,128]{1,0:T(8,128)}) %reduce-scatter.2.cloned.1.call-update) | async-done | bytes 262160 | tf_op jit(solution)/shard_map/reduce_scatter | solution.py:104
  775.3 1.6 convert_element_type.37
  776.9 651.3 %all-reduce.5.cloned.1.call-done = f32[128,512]{1,0:T(8,128)} async-done(((f32[128,512]{1,0:T(8,128)}), f32[128,512]{1,0:T(8,128)}) %all-reduce.5.cloned.1.call-update) | async-done | bytes 262160 | tf_op jit(solution)/shard_map/psum | solution.py:90
  1428.2 1.7 copy.40
  (56 shorter events, 12.5 us)
Async XLA Ops:
  7.2 268.5 %copy-start = (bf16[128,512]{1,0:T(8,128)(2,1)S(1)}, bf16[128,512]{1,0:T(8,128)(2,1)}, u32[]{:S(2)}) copy-start(bf16[128,512]{1,0:T(8,128)(2,1)} %param.15) | copy-start | bytes 393220
  12.7 25.8 %all-to-all-start = ((s32[64,1,16]{2,1,0:T(1,128)}), s32[64,1,16]{2,1,0:T(1,128)S(1)}, u32[]{:S(2)}, u32[]{:S(2)}) async-start(s32[64,1,16]{2,1,0:T(1,128)} %bitcast.4), calls=%async_computation | async-start | bytes 65536 | tf_op jit(solution)/shard_map/all_to_all | solution.py:39
  38.5 17.2 %all-to-all-start.1 = ((bf16[64,16,128]{2,1,0:T(8,128)(2,1)}), bf16[64,16,128]{2,1,0:T(8,128)(2,1)S(1)}, u32[]{:S(2)}, u32[]{:S(2)}) async-start(bf16[64,16,128]{2,1,0:T(8,128)(2,1)} %bitcast.6), calls=%async_computation.1 | async-start | bytes 524288 | tf_op jit(solution)/shard_map/all_to_all | solution.py:38
  43.1 157.1 %all-gather.2.cloned.1.call-start = ((), (), s32[]{:S(2)}) async-start(), calls=%async_computation.3 | async-start | bytes 8519680 | tf_op jit(solution)/shard_map/all_gather | solution.py:64
  59.4 263.8 %all-reduce.3.cloned.1.call-start = ((), (), s32[]{:S(2)}) async-start(), calls=%async_computation.4 | async-start | bytes 2097152 | tf_op jit(solution)/shard_map/psum | solution.py:78
  242.5 34.8 %copy-start.3 = (s32[1,64,4]{1,2,0:T(4,128)S(1)}, s32[1,64,4]{1,2,0:T(4,128)}, u32[]{:S(2)}) copy-start(s32[1,64,4]{1,2,0:T(4,128)} %param.12) | copy-start | bytes 3076
  242.5 80.7 %copy-start.2 = (bf16[512,512]{1,0:T(8,128)(2,1)S(1)}, bf16[512,512]{1,0:T(8,128)(2,1)}, u32[]{:S(2)}) copy-start(bf16[512,512]{1,0:T(8,128)(2,1)} %param.17) | copy-start | bytes 1572868
  242.5 80.7 %copy-start.4 = (f32[512]{0:T(512)S(1)}, f32[512]{0:T(512)}, u32[]{:S(2)}) copy-start(f32[512]{0:T(512)} %param.16) | copy-start | bytes 6148
  277.0 498.3 %reduce-scatter.2.cloned.1.call-start = ((), (), s32[]{:S(2)}) async-start(), calls=%async_computation.6 | async-start | bytes 17039360 | tf_op jit(solution)/shard_map/reduce_scatter | solution.py:104
  422.0 1007.9 %copy-start.1 = (bf16[128,512]{1,0:T(8,128)(2,1)S(1)}, bf16[128,512]{1,0:T(8,128)(2,1)}, u32[]{:S(2)}) copy-start(bf16[128,512]{1,0:T(8,128)(2,1)} %param.15) | copy-start | bytes 393220
  422.0 1006.1 %all-reduce.5.cloned.1.call-start = ((), (), s32[]{:S(2)}) async-start(), calls=%async_computation.5 | async-start | bytes 524288 | tf_op jit(solution)/shard_map/psum | solution.py:90
Sparse Core Ops, SparseCore 0:
  59.5 140.5 all-gather.1
  277.1 46.0 all-reduce.2
  422.2 353.1 reduce-scatter.1
  778.5 649.5 all-reduce.4
where the time goes:
time: 1470 us; the launch traced here: 1440 us
  waiting for transfers between devices  1040 us (71%)
  blocking collectives  164 us (11%)
  other arithmetic  90.2 us (6%)
  local copies, waits for them, and re-layouts  78 us (5%)
  matrix products  29.8 us (2%)
  starting transfers between devices  20.3 us (1%)
    psum x1, waiting for transfers between devices, per_device(): weight_grad, bias_grad = lax.psum((weight_part, bias_part), 'blk')  651 us
    reduce_scatter x1, waiting for transfers between devices, per_device(): lax.psum_scatter(place_tiles(product, column, live, span_count * row_tile...  187 us
    psum x1, blocking collectives, per_device(): weight_grad, bias_grad = lax.psum((weight_part, bias_part), 'blk')  164 us
    all_gather x1, waiting for transfers between devices, per_device(): piece = lax.all_gather(regrouped, 'blk', axis=0, tiled=True)  137 us
    scatter-add x2, other arithmetic, place_tiles(): placed = jnp.zeros((total, tile_size, column_share), jnp.float32).at[wher...  81.6 us
    psum x1, waiting for transfers between devices, per_device(): pre = lax.psum(partial_pre, 'rep') + layer_bias  45.7 us
    reshape x2, local copies, waits for them, and re-layouts, place_tiles(): flat = product.reshape(-1, tile_size, column_share)  34.9 us
  transfers between devices with their start and end apart: 6, of which 6 were waited for; matrix products, arithmetic and copies ran while one was open for 1% of the time, Pallas kernels for 0%

commit v1 on v0

v1 whole, which is shorter than its diff:
```python
import jax
import jax.numpy as jnp
from jax import lax
from jax.sharding import PartitionSpec as P

PARTNERS = 6
BF = jnp.bfloat16
F32 = jnp.float32


def one_hot(condition):
    return condition.astype(BF)


def dot(a, b, dims=((1,), (0,))):
    return lax.dot_general(a, b, (dims, ((), ())), preferred_element_type=F32)


def exchange(x):
    return lax.all_to_all(x, "blk", split_axis=0, concat_axis=0, tiled=True)


def per_device(
    features,
    row_target,
    tile_values,
    tile_rows,
    tile_cols,
    tile_counts,
    weight,
    layer_bias,
    out_grad,
):
    blocks = lax.axis_size("blk")
    members = lax.axis_size("rep")
    me = lax.axis_index("blk")
    member = lax.axis_index("rep")
    rows, cols = features.shape
    slots, tile = tile_values.shape[2:4]
    tiles = rows // tile
    bucket = 2 * rows // blocks
    piece = rows // blocks

    full_weight = lax.all_gather(weight, "rep", axis=0, tiled=True)
    all_counts = lax.all_gather(tile_counts[0], "blk", axis=0).reshape(blocks, blocks)

    ids = jnp.arange(blocks, dtype=jnp.int32)
    target = row_target // rows
    landing = row_target % rows
    hits = target[None, :] == ids[:, None]
    at = jnp.arange(rows, dtype=jnp.int32)
    earlier = dot(one_hot(hits), one_hot(at[:, None] < at[None, :]))
    rank = jnp.sum(jnp.where(hits, earlier, 0.0), axis=0).astype(jnp.int32)
    slot = target * bucket + rank
    to_slot = slot[None, :] == jnp.arange(blocks * bucket, dtype=jnp.int32)[:, None]
    send_rows = dot(one_hot(to_slot), features).astype(BF)
    send_where = jnp.sum(jnp.where(to_slot, landing[None, :] + 1, 0), axis=1) - 1
    got_rows = exchange(send_rows.reshape(blocks, bucket, cols)).reshape(-1, cols)
    got_where = exchange(send_where.reshape(blocks, bucket)).reshape(-1)
    regrouped = dot(one_hot(got_where[None, :] == at[:, None]), got_rows).astype(BF)

    partner = (all_counts > 0) & (ids[:, None] != ids[None, :])
    order = dot(one_hot(partner), one_hot(ids[:, None] < ids[None, :]))
    wanted = jnp.arange(PARTNERS, dtype=F32)
    choose = partner[:, None, :] & (order[:, None, :] == wanted[None, :, None])
    flat_choose = one_hot(choose).reshape(blocks * PARTNERS, blocks)
    mine = lax.dynamic_index_in_dim(choose, me, 0, keepdims=False)
    mine = jnp.concatenate([mine, (ids == me)[None]], axis=0).astype(jnp.int32)
    which = jnp.sum(mine * ids[None, :], axis=1)
    meets = PARTNERS + 1

    row_of = jnp.sum(mine[:, :, None] * tile_rows[0][None], axis=1)
    col_of = jnp.sum(mine[:, :, None] * tile_cols[0][None], axis=1)
    live = jnp.sum(mine * tile_counts[0][None], axis=1)
    live = jnp.arange(slots, dtype=jnp.int32)[None, :] < live[:, None]
    tile_ids = jnp.arange(tiles, dtype=jnp.int32)
    spot = (
        live[:, :, None, None]
        & (row_of[:, :, None, None] == tile_ids[None, None, :, None])
        & (col_of[:, :, None, None] == tile_ids[None, None, None, :])
    )
    adjacency = []
    for k in range(meets):
        values = lax.dynamic_index_in_dim(tile_values[0], which[k], 0, keepdims=False)
        dense = jnp.zeros((tiles, tile, tiles, tile), BF)
        for s in range(slots):
            dense = jnp.where(
                spot[k, s][:, None, :, None], values[s][None, :, None, :], dense
            )
        adjacency.append(dense.reshape(rows, rows))
    adjacency = jnp.concatenate(adjacency, axis=1)

    spread = exchange(regrouped.reshape(blocks, piece, cols)).reshape(blocks, piece * cols)
    served = dot(flat_choose, spread).astype(BF)
    served = exchange(served.reshape(blocks, PARTNERS * piece, cols))
    served = served.reshape(blocks, PARTNERS, piece, cols).transpose(1, 0, 2, 3)
    inputs = jnp.concatenate([served.reshape(PARTNERS * rows, cols), regrouped], axis=0)
    mixed = dot(adjacency, inputs).astype(BF)

    full_mixed = lax.all_gather(mixed, "rep", axis=1, tiled=True)
    pre = dot(full_mixed, full_weight) + layer_bias
    sigma = jax.nn.sigmoid(pre)
    share = rows // members
    output = lax.dynamic_slice_in_dim((pre * sigma).astype(BF), member * share, share, 0)
    pre_grad = (out_grad.astype(F32) * sigma * (1.0 + pre * (1.0 - sigma))).astype(BF)
    mixed_grad = dot(pre_grad, weight, ((1,), (1,))).astype(BF)

    terms = dot(adjacency, mixed_grad, ((0,), (0,)))
    own = terms[PARTNERS * rows :]
    away = terms[: PARTNERS * rows].astype(BF).reshape(PARTNERS, blocks, piece, cols)
    away = exchange(away.transpose(1, 0, 2, 3).reshape(blocks, PARTNERS * piece, cols))
    away = away.reshape(blocks * PARTNERS, piece * cols)
    summed = dot(flat_choose, away, ((0,), (0,)))
    back = exchange(summed.reshape(blocks, piece, cols)).reshape(rows, cols)
    feature_grad = (back + own).astype(BF)

    weight_part = dot(mixed, pre_grad, ((0,), (0,)))
    bias_part = jnp.sum(pre_grad.astype(F32), axis=0)
    bias_grad = jnp.sum(lax.all_gather(bias_part, "blk", axis=0), axis=0)
    wide = weight_part.shape[1]
    weight_part = exchange(weight_part.reshape(blocks, -1, wide))
    weight_grad = lax.all_gather(jnp.sum(weight_part, axis=0), "blk", axis=0, tiled=True)
    return (output, weight_grad, bias_grad, feature_grad)


def solution(mesh):
    in_specs = (
        P("blk", "rep"),
        P("blk"),
        P("blk", None, None, None, None),
        P("blk", None, None),
        P("blk", None, None),
        P("blk", None),
        P("rep", None),
        P(),
        P("blk", None),
    )
    out_specs = (P(("blk", "rep"), None), P("rep", None), P(), P("blk", "rep"))
    return jax.shard_map(
        per_device, mesh=mesh, in_specs=in_specs, out_specs=out_specs, check_vma=False
    )
```

time: 1470 us -> 726 us (0.49)
  the two profiles are of different devices: /device:TPU:1 before, /device:TPU:32 now
where the time goes in v1:
time: 726 us; the launch traced here: 725 us
  blocking collectives  547 us (75%)
  starting transfers between devices  58.2 us (8%)
  waiting for transfers between devices  57.9 us (8%)
  local copies, waits for them, and re-layouts  17.3 us (2%)
  matrix products  16.1 us (2%)
  between operations  14.3 us (2%)
  other arithmetic  13.6 us (2%)
    all_gather x1, blocking collectives, per_device(): lax.all_gather(jnp.sum(weight_part, axis=0), 'blk', axis=0, tiled=True)  181 us
    all_gather x1, blocking collectives, per_device(): bias_grad = jnp.sum(lax.all_gather(bias_part, 'blk', axis=0), axis=0)  177 us
    all_gather x1, blocking collectives, per_device(): lax.all_gather(tile_counts[0], 'blk', axis=0).reshape(blocks, blocks)  175 us
    all_to_all x7, starting transfers between devices, exchange(): return lax.all_to_all(x, 'blk', split_axis=0, concat_axis=0, tiled=True)  58.2 us
    all_to_all x7, waiting for transfers between devices, exchange(): return lax.all_to_all(x, 'blk', split_axis=0, concat_axis=0, tiled=True)  57.9 us
    dot_general x10, matrix products, dot(): return lax.dot_general(a, b, (dims, ((), ())), preferred_element_type=F32)  16.1 us
  transfers between devices with their start and end apart: 7, of which 5 were waited for; matrix products, arithmetic and copies ran while one was open for 4% of the time, Pallas kernels for 0%

profile of v1, /device:TPU:32, one launch (start us, length us, event | category | flops | bytes accessed | tf_op | source)
XLA Modules:
  0.0 724.9 jit_solution(7916404086749864458)
XLA Ops:
  2.6 14.2 %all-to-all-start = ((s32[64,1,16]{2,1,0:T(1,128)}), s32[64,1,16]{2,1,0:T(1,128)S(1)}, u32[]{:S(2)}, u32[]{:S(2)}) async-start(s32[64,1,16]{2,1,0:T(1,128)} %bitcast.70), calls=%async_computation | async-start | bytes 65536 | tf_op jit(solution)/shard_map/all_to_all | solution.py:20
  16.8 175.0 %all-gather.1 = s32[64,1,64]{2,1,0:T(1,128)S(1)} all-gather(s32[1,1,64]{2,1,0:T(1,128)} %bitcast.215), channel_id=1, replica_groups=mesh['blk'=64,'rep'=4] {'blk'}, dimensions={0}, use_global_device_ids=true | all-gather | bytes 16640 | tf_op jit(solution)/shard_map/all_gather | solution.py:45
  208.9 2.0 dynamic-slice_bitcast_fusion.3
  213.5 11.2 %all-to-all-start.1 = ((bf16[64,16,128]{2,1,0:T(8,128)(2,1)}), bf16[64,16,128]{2,1,0:T(8,128)(2,1)}, u32[]{:S(2)}, u32[]{:S(2)}) async-start(bf16[64,16,128]{2,1,0:T(8,128)(2,1)} %bitcast.71), calls=%async_computation.1 | async-start | bytes 524288 | tf_op jit(solution)/shard_map/all_to_all | solution.py:20
  227.3 1.5 reduce.4
  228.9 9.0 %all-to-all-done.1 = bf16[64,16,128]{2,1,0:T(8,128)(2,1)} async-done(((bf16[64,16,128]{2,1,0:T(8,128)(2,1)}), bf16[64,16,128]{2,1,0:T(8,128)(2,1)}, u32[]{:S(2)}, u32[]{:S(2)}) %all-to-all-start.1) | async-done | bytes 262176 | tf_op jit(solution)/shard_map/all_to_all | solution.py:20
  237.9 2.1 fusion.3
  240.0 5.7 all-to-all-start.2
  248.5 9.1 %all-to-all-done.2 = bf16[64,8,128]{2,1,0:T(8,128)(2,1)} async-done(((bf16[64,8,128]{2,1,0:T(8,128)(2,1)}), bf16[64,8,128]{2,1,0:T(8,128)(2,1)}, u32[]{:S(2)}, u32[]{:S(2)}) %all-to-all-start.2) | async-done | bytes 131104 | tf_op jit(solution)/shard_map/all_to_all | solution.py:20
  260.2 5.3 all-to-all-start.3
  265.4 8.0 %all_gather.20 = bf16[512,512]{1,0:T(8,128)(2,1)} all-gather(bf16[128,512]{1,0:T(8,128)(2,1)} %param.15), channel_id=1, replica_groups=mesh['blk'=64,'rep'=4] {'rep'}, dimensions={0}, use_global_device_ids=true | all-gather | bytes 655360 | tf_op jit(solution)/shard_map/all_gather | solution.py:44
  278.8 4.9 all-to-all-done.3
  283.9 3.2 convolution_convert_fusion.2
  287.1 6.5 all_gather.19
  293.7 2.1 convert_reduce_fusion
  295.8 3.6 fusion.4
  300.5 11.0 %all-to-all-start.5 = ((bf16[64,48,128]{2,1,0:T(8,128)(2,1)}), bf16[64,48,128]{2,1,0:T(8,128)(2,1)S(1)}, u32[]{:S(2)}, u32[]{:S(2)}) async-start(bf16[64,48,128]{2,1,0:T(8,128)(2,1)} %bitcast.198), calls=%async_computation.5 | async-start | bytes 1572864 | tf_op jit(solution)/shard_map/all_to_all | solution.py:20
  313.5 23.8 %all-to-all-done.5 = bf16[64,48,128]{2,1,0:T(8,128)(2,1)S(1)} async-done(((bf16[64,48,128]{2,1,0:T(8,128)(2,1)}), bf16[64,48,128]{2,1,0:T(8,128)(2,1)S(1)}, u32[]{:S(2)}, u32[]{:S(2)}) %all-to-all-start.5) | async-done | bytes 786464 | tf_op jit(solution)/shard_map/all_to_all | solution.py:20
  337.3 5.8 all-to-all-start.4
  345.8 11.0 %all-to-all-done.4 = f32[64,2,512]{2,1,0:T(2,128)} async-done(((f32[64,2,512]{2,1,0:T(2,128)}), f32[64,2,512]{2,1,0:T(2,128)}, u32[]{:S(2)}, u32[]{:S(2)}) %all-to-all-start.4) | async-done | bytes 262176 | tf_op jit(solution)/shard_map/all_to_all | solution.py:20
  356.8 5.1 all-to-all-start.6
  361.9 176.7 %all-gather.3 = f32[64,1,512]{2,1,0:T(1,128)S(1)} all-gather(f32[1,1,512]{2,1,0:T(1,128)S(1)} %bitcast.214), channel_id=2, replica_groups=mesh['blk'=64,'rep'=4] {'blk'}, dimensions={0}, use_global_device_ids=true | all-gather | bytes 133120 | tf_op jit(solution)/shard_map/all_gather | solution.py:119
  539.3 1.7 fusion.12
  542.1 181.3 %all-gather.2 = f32[64,2,512]{2,1,0:T(2,128)S(1)} all-gather(f32[1,2,512]{2,1,0:T(2,128)S(1)} %bitcast.213), channel_id=1, replica_groups=mesh['blk'=64,'rep'=4] {'blk'}, dimensions={0}, use_global_device_ids=true | all-gather | bytes 266240 | tf_op jit(solution)/shard_map/all_gather | solution.py:122
  (73 shorter events, 30.8 us)
Async XLA Ops:
  0.6 211.6 %copy-start = (bf16[512,128]{1,0:T(8,128)(2,1)S(1)}, bf16[512,128]{1,0:T(8,128)(2,1)}, u32[]{:S(2)}) copy-start(bf16[512,128]{1,0:T(8,128)(2,1)} %param.9) | copy-start | bytes 393220
  2.6 210.9 %all-to-all-start = ((s32[64,1,16]{2,1,0:T(1,128)}), s32[64,1,16]{2,1,0:T(1,128)S(1)}, u32[]{:S(2)}, u32[]{:S(2)}) async-start(s32[64,1,16]{2,1,0:T(1,128)} %bitcast.70), calls=%async_computation | async-start | bytes 65536 | tf_op jit(solution)/shard_map/all_to_all | solution.py:20
  213.5 11.2 %copy-start.6 = (s32[64,1,16]{2,1,0:T(1,128)}, s32[64,1,16]{2,1,0:T(1,128)S(1)}, u32[]{:S(2)}) copy-start(s32[64,1,16]{2,1,0:T(1,128)S(1)} %all-to-all-done) | copy-start | bytes 12292
  213.5 24.4 %all-to-all-start.1 = ((bf16[64,16,128]{2,1,0:T(8,128)(2,1)}), bf16[64,16,128]{2,1,0:T(8,128)(2,1)}, u32[]{:S(2)}, u32[]{:S(2)}) async-start(bf16[64,16,128]{2,1,0:T(8,128)(2,1)} %bitcast.71), calls=%async_computation.1 | async-start | bytes 524288 | tf_op jit(solution)/shard_map/all_to_all | solution.py:20
  240.0 17.7 %all-to-all-start.2 = ((bf16[64,8,128]{2,1,0:T(8,128)(2,1)}), bf16[64,8,128]{2,1,0:T(8,128)(2,1)}, u32[]{:S(2)}, u32[]{:S(2)}) async-start(bf16[64,8,128]{2,1,0:T(8,128)(2,1)} %bitcast.212), calls=%async_computation.2 | async-start | bytes 262144 | tf_op jit(solution)/shard_map/all_to_all | solution.py:20
  260.2 23.6 %all-to-all-start.3 = ((bf16[64,48,128]{2,1,0:T(8,128)(2,1)}), bf16[64,48,128]{2,1,0:T(8,128)(2,1)S(1)}, u32[]{:S(2)}, u32[]{:S(2)}) async-start(bf16[64,48,128]{2,1,0:T(8,128)(2,1)} %reshape.423), calls=%async_computation.3 | async-start | bytes 1572864 | tf_op jit(solution)/shard_map/all_to_all | solution.py:20
  265.4 12.4 %copy-start.1 = (bf16[4,128,4,128]{3,2,1,0:T(4,128)(2,1)S(1)}, bf16[4,128,4,128]{3,2,1,0:T(4,128)(2,1)}, u32[]{:S(2)}) copy-start(bf16[4,128,4,128]{3,2,1,0:T(4,128)(2,1)} %select_select_fusion) | copy-start | bytes 1572868
  274.3 9.6 %copy-start.5 = (bf16[512,128]{1,0:T(8,128)(2,1)S(1)}, bf16[512,128]{1,0:T(8,128)(2,1)}, u32[]{:S(2)}) copy-start(bf16[512,128]{1,0:T(8,128)(2,1)} %fusion.3) | copy-start | bytes 393220
  283.7 9.9 %copy-start.4 = (bf16[512,512]{1,0:T(8,128)(2,1)S(1)}, bf16[512,512]{1,0:T(8,128)(2,1)}, u32[]{:S(2)}) copy-start(bf16[512,512]{1,0:T(8,128)(2,1)} %all_gather.20) | copy-start | bytes 1572868
  283.7 9.9 %copy-start.7 = (bf16[512,512]{1,0:T(8,128)(2,1)S(1)}, bf16[512,512]{1,0:T(8,128)(2,1)}, u32[]{:S(2)}) copy-start(bf16[512,512]{1,0:T(8,128)(2,1)} %param.17) | copy-start | bytes 1572868
  283.7 9.9 %copy-start.8 = (f32[512]{0:T(512)S(1)}, f32[512]{0:T(512)}, u32[]{:S(2)}) copy-start(f32[512]{0:T(512)} %param.16) | copy-start | bytes 6148
  287.1 8.7 %copy-start.3 = (bf16[512,128]{1,0:T(8,128)(2,1)}, bf16[512,128]{1,0:T(8,128)(2,1)S(1)}, u32[]{:S(2)}) copy-start(bf16[512,128]{1,0:T(8,128)(2,1)S(1)} %convolution_convert_fusion.2) | copy-start | bytes 393220
  293.7 2.1 copy-start.2
  300.5 36.8 %all-to-all-start.5 = ((bf16[64,48,128]{2,1,0:T(8,128)(2,1)}), bf16[64,48,128]{2,1,0:T(8,128)(2,1)S(1)}, u32[]{:S(2)}, u32[]{:S(2)}) async-start(bf16[64,48,128]{2,1,0:T(8,128)(2,1)} %bitcast.198), calls=%async_computation.5 | async-start | bytes 1572864 | tf_op jit(solution)/shard_map/all_to_all | solution.py:20
  337.3 19.5 %all-to-all-start.4 = ((f32[64,2,512]{2,1,0:T(2,128)}), f32[64,2,512]{2,1,0:T(2,128)}, u32[]{:S(2)}, u32[]{:S(2)}) async-start(f32[64,2,512]{2,1,0:T(2,128)} %reshape.426), calls=%async_computation.4 | async-start | bytes 524288 | tf_op jit(solution)/shard_map/all_to_all | solution.py:20
  356.8 367.4 %all-to-all-start.6 = ((f32[64,8,128]{2,1,0:T(8,128)}), f32[64,8,128]{2,1,0:T(8,128)S(1)}, u32[]{:S(2)}, u32[]{:S(2)}) async-start(f32[64,8,128]{2,1,0:T(8,128)} %copy.50), calls=%async_computation.6 | async-start | bytes 524288 | tf_op jit(solution)/shard_map/all_to_all | solution.py:20

commit v2 on v1

--- a/solution.py
+++ b/solution.py
@@ -18,6 +18,10 @@
 
 def exchange(x):
     return lax.all_to_all(x, "blk", split_axis=0, concat_axis=0, tiled=True)
+
+
+def everywhere(x, blocks):
+    return exchange(jnp.broadcast_to(x[None], (blocks, *x.shape)))
 
 
 def per_device(
@@ -42,7 +46,7 @@
     piece = rows // blocks
 
     full_weight = lax.all_gather(weight, "rep", axis=0, tiled=True)
-    all_counts = lax.all_gather(tile_counts[0], "blk", axis=0).reshape(blocks, blocks)
+    all_counts = everywhere(tile_counts[0], blocks)
 
     ids = jnp.arange(blocks, dtype=jnp.int32)
     target = row_target // rows
@@ -116,10 +120,12 @@
 
     weight_part = dot(mixed, pre_grad, ((0,), (0,)))
     bias_part = jnp.sum(pre_grad.astype(F32), axis=0)
-    bias_grad = jnp.sum(lax.all_gather(bias_part, "blk", axis=0), axis=0)
     wide = weight_part.shape[1]
     weight_part = exchange(weight_part.reshape(blocks, -1, wide))
-    weight_grad = lax.all_gather(jnp.sum(weight_part, axis=0), "blk", axis=0, tiled=True)
+    weight_sum = jnp.sum(weight_part, axis=0)
+    bias_terms = everywhere(bias_part[None], blocks)
+    weight_grad = everywhere(weight_sum, blocks).reshape(weight.shape)
+    bias_grad = jnp.sum(bias_terms, axis=(0, 1))
     return (output, weight_grad, bias_grad, feature_grad)
 
 

time: 726 us -> 255 us (0.35)
  the two profiles are of different devices: /device:TPU:32 before, /device:TPU:1 now
where the time goes in v2:
time: 255 us; the launch traced here: 251 us
  waiting for transfers between devices  88 us (35%)
  starting transfers between devices  78.3 us (31%)
  local copies, waits for them, and re-layouts  21.7 us (9%)
  blocking collectives  21.3 us (8%)
  matrix products  14.3 us (6%)
  between operations  14.2 us (6%)
  other arithmetic  12.7 us (5%)
    all_to_all x10, waiting for transfers between devices, exchange(): return lax.all_to_all(x, 'blk', split_axis=0, concat_axis=0, tiled=True)  88 us
    all_to_all x10, starting transfers between devices, exchange(): return lax.all_to_all(x, 'blk', split_axis=0, concat_axis=0, tiled=True)  78.3 us
    dot_general x10, matrix products, dot(): return lax.dot_general(a, b, (dims, ((), ())), preferred_element_type=F32)  14.3 us
    all_gather x1, blocking collectives, per_device(): full_mixed = lax.all_gather(mixed, 'rep', axis=1, tiled=True)  12.7 us
    all_gather x1, blocking collectives, per_device(): full_weight = lax.all_gather(weight, 'rep', axis=0, tiled=True)  8.61 us
    unnamed x18, local copies, waits for them, and re-layouts  6.01 us
  transfers between devices with their start and end apart: 10, of which 9 were waited for; matrix products, arithmetic and copies ran while one was open for 13% of the time, Pallas kernels for 0%

profile of v2, /device:TPU:1, one launch (start us, length us, event | category | flops | bytes accessed | tf_op | source)
XLA Modules:
  0.0 250.5 jit_solution(12039082956160871963)
XLA Ops:
  2.6 15.1 %all-to-all-start.1 = ((s32[64,1,16]{2,1,0:T(1,128)}), s32[64,1,16]{2,1,0:T(1,128)S(1)}, u32[]{:S(2)}, u32[]{:S(2)}) async-start(s32[64,1,16]{2,1,0:T(1,128)} %bitcast.70), calls=%async_computation.1 | async-start | bytes 65536 | tf_op jit(solution)/shard_map/all_to_all | solution.py:20
  18.9 8.6 %all_gather.7 = bf16[512,512]{1,0:T(8,128)(2,1)} all-gather(bf16[128,512]{1,0:T(8,128)(2,1)} %param.15), channel_id=1, replica_groups=mesh['blk'=64,'rep'=4] {'rep'}, dimensions={0}, use_global_device_ids=true | all-gather | bytes 655360 | tf_op jit(solution)/shard_map/all_gather | solution.py:48
  29.7 11.7 %all-to-all-start = ((s32[64,1,64]{2,1,0:T(1,128)}), s32[64,1,64]{2,1,0:T(1,128)S(1)}, u32[]{:S(2)}, u32[]{:S(2)}) async-start(s32[64,1,64]{2,1,0:T(1,128)} %broadcast_in_dim.457), calls=%async_computation | async-start | bytes 65536 | tf_op jit(solution)/shard_map/all_to_all | solution.py:20
  42.8 9.3 %all-to-all-done = s32[64,1,64]{2,1,0:T(1,128)S(1)} async-done(((s32[64,1,64]{2,1,0:T(1,128)}), s32[64,1,64]{2,1,0:T(1,128)S(1)}, u32[]{:S(2)}, u32[]{:S(2)}) %all-to-all-start) | async-done | bytes 16416 | tf_op jit(solution)/shard_map/all_to_all | solution.py:20
  52.1 4.6 %all-to-all-start.2 = ((bf16[64,16,128]{2,1,0:T(8,128)(2,1)}), bf16[64,16,128]{2,1,0:T(8,128)(2,1)S(1)}, u32[]{:S(2)}, u32[]{:S(2)}) async-start(bf16[64,16,128]{2,1,0:T(8,128)(2,1)} %bitcast.71), calls=%async_computation.2 | async-start | bytes 524288 | tf_op jit(solution)/shard_map/all_to_all | solution.py:20
  73.6 2.1 dynamic-slice_bitcast_fusion.3
  79.1 12.5 %all-to-all-start.3 = ((bf16[64,8,128]{2,1,0:T(8,128)(2,1)}), bf16[64,8,128]{2,1,0:T(8,128)(2,1)}, u32[]{:S(2)}, u32[]{:S(2)}) async-start(bf16[64,8,128]{2,1,0:T(8,128)(2,1)} %bitcast.73), calls=%async_computation.3 | async-start | bytes 262144 | tf_op jit(solution)/shard_map/all_to_all | solution.py:20
  94.3 8.7 %all-to-all-done.3 = bf16[64,8,128]{2,1,0:T(8,128)(2,1)} async-done(((bf16[64,8,128]{2,1,0:T(8,128)(2,1)}), bf16[64,8,128]{2,1,0:T(8,128)(2,1)}, u32[]{:S(2)}, u32[]{:S(2)}) %all-to-all-start.3) | async-done | bytes 131104 | tf_op jit(solution)/shard_map/all_to_all | solution.py:20
  105.4 4.8 %all-to-all-start.4 = ((bf16[64,48,128]{2,1,0:T(8,128)(2,1)}), bf16[64,48,128]{2,1,0:T(8,128)(2,1)S(1)}, u32[]{:S(2)}, u32[]{:S(2)}) async-start(bf16[64,48,128]{2,1,0:T(8,128)(2,1)} %reshape.452), calls=%async_computation.4 | async-start | bytes 1572864 | tf_op jit(solution)/shard_map/all_to_all | solution.py:20
  116.9 12.9 %all-to-all-done.4 = bf16[64,48,128]{2,1,0:T(8,128)(2,1)S(1)} async-done(((bf16[64,48,128]{2,1,0:T(8,128)(2,1)}), bf16[64,48,128]{2,1,0:T(8,128)(2,1)S(1)}, u32[]{:S(2)}, u32[]{:S(2)}) %all-to-all-start.4) | async-done | bytes 786464 | tf_op jit(solution)/shard_map/all_to_all | solution.py:20
  129.9 3.2 %convolution_convert_fusion.2 = bf16[512,128]{1,0:T(8,128)(2,1)S(1)} fusion(bf16[512,3584]{1,0:T(8,128)(2,1)} %bitcast_dynamic-update-slice_fusion, bf16[512,128]{1,0:T(8,128)(2,1)} %fusion.3, bf16[3072,128]{1,0:T(8,128)(2,1)S(1)} %bitcast.211), kind=kOutput, calls=%fused_computation.11 | convolution fusion | flops 471662592 | bytes 4718592 | tf_op jit(solution)/shard_map/dot_general | solution.py:16
  133.2 12.7 %all_gather.6 = bf16[512,512]{1,0:T(8,128)(2,1)S(1)} all-gather(bf16[512,128]{1,0:T(8,128)(2,1)S(1)} %convolution_convert_fusion.2), channel_id=1, replica_groups=mesh['blk'=64,'rep'=4] {'rep'}, dimensions={1}, use_global_device_ids=true | all-gather | bytes 655360 | tf_op jit(solution)/shard_map/all_gather | solution.py:104
  145.9 2.1 convert_reduce_fusion
  148.8 5.5 %all-to-all-start.7 = ((f32[64,1,512]{2,1,0:T(1,128)}), f32[64,1,512]{2,1,0:T(1,128)S(1)}, u32[]{:S(2)}, u32[]{:S(2)}) async-start(f32[64,1,512]{2,1,0:T(1,128)} %broadcast_in_dim.574), calls=%async_computation.7 | async-start | bytes 262144 | tf_op jit(solution)/shard_map/all_to_all | solution.py:20
  155.4 10.8 %all-to-all-done.7 = f32[64,1,512]{2,1,0:T(1,128)S(1)} async-done(((f32[64,1,512]{2,1,0:T(1,128)}), f32[64,1,512]{2,1,0:T(1,128)S(1)}, u32[]{:S(2)}, u32[]{:S(2)}) %all-to-all-start.7) | async-done | bytes 131104 | tf_op jit(solution)/shard_map/all_to_all | solution.py:20
  166.8 4.6 %all-to-all-start.5 = ((f32[64,2,512]{2,1,0:T(2,128)}), f32[64,2,512]{2,1,0:T(2,128)S(1)}, u32[]{:S(2)}, u32[]{:S(2)}) async-start(f32[64,2,512]{2,1,0:T(2,128)} %reshape.455), calls=%async_computation.5 | async-start | bytes 524288 | tf_op jit(solution)/shard_map/all_to_all | solution.py:20
  171.5 3.6 %fusion.4 = f32[3584,128]{1,0:T(8,128)S(1)} fusion(bf16[512,3584]{1,0:T(8,128)(2,1)} %bitcast_dynamic-update-slice_fusion, bf16[512,512]{1,0:T(8,128)(2,1)S(1)} %get-tuple-element.9, bf16[128,512]{1,0:T(8,128)(2,1)S(1)} %copy-done.1), kind=kOutput, calls=%fused_computation.13 | convolution fusion | flops 536936448 | bytes 6160384 | tf_op jit(solution)/shard_map/dot_general | solution.py:16
  176.2 7.8 %all-to-all-done.5 = f32[64,2,512]{2,1,0:T(2,128)S(1)} async-done(((f32[64,2,512]{2,1,0:T(2,128)}), f32[64,2,512]{2,1,0:T(2,128)S(1)}, u32[]{:S(2)}, u32[]{:S(2)}) %all-to-all-start.5) | async-done | bytes 262176 | tf_op jit(solution)/shard_map/all_to_all | solution.py:20
  184.0 6.0 %all-to-all-start.8 = ((bf16[64,48,128]{2,1,0:T(8,128)(2,1)}), bf16[64,48,128]{2,1,0:T(8,128)(2,1)S(1)}, u32[]{:S(2)}, u32[]{:S(2)}) async-start(bf16[64,48,128]{2,1,0:T(8,128)(2,1)} %bitcast.199), calls=%async_computation.8 | async-start | bytes 1572864 | tf_op jit(solution)/shard_map/all_to_all | solution.py:20
  190.1 20.6 %all-to-all-done.8 = bf16[64,48,128]{2,1,0:T(8,128)(2,1)S(1)} async-done(((bf16[64,48,128]{2,1,0:T(8,128)(2,1)}), bf16[64,48,128]{2,1,0:T(8,128)(2,1)S(1)}, u32[]{:S(2)}, u32[]{:S(2)}) %all-to-all-start.8) | async-done | bytes 786464 | tf_op jit(solution)/shard_map/all_to_all | solution.py:20
  211.4 8.9 %all-to-all-start.6 = ((f32[64,2,512]{2,1,0:T(2,128)}), f32[64,2,512]{2,1,0:T(2,128)}, u32[]{:S(2)}, u32[]{:S(2)}) async-start(f32[64,2,512]{2,1,0:T(2,128)} %broadcast_in_dim.573), calls=%async_computation.6 | async-start | bytes 524288 | tf_op jit(solution)/shard_map/all_to_all | solution.py:20
  223.1 9.6 %all-to-all-done.6 = f32[64,2,512]{2,1,0:T(2,128)} async-done(((f32[64,2,512]{2,1,0:T(2,128)}), f32[64,2,512]{2,1,0:T(2,128)}, u32[]{:S(2)}, u32[]{:S(2)}) %all-to-all-start.6) | async-done | bytes 262176 | tf_op jit(solution)/shard_map/all_to_all | solution.py:20
  232.7 4.6 %all-to-all-start.9 = ((f32[64,8,128]{2,1,0:T(8,128)}), f32[64,8,128]{2,1,0:T(8,128)S(1)}, u32[]{:S(2)}, u32[]{:S(2)}) async-start(f32[64,8,128]{2,1,0:T(8,128)} %copy.65), calls=%async_computation.9 | async-start | bytes 524288 | tf_op jit(solution)/shard_map/all_to_all | solution.py:20
  242.5 7.4 %all-to-all-done.9 = f32[64,8,128]{2,1,0:T(8,128)S(1)} async-done(((f32[64,8,128]{2,1,0:T(8,128)}), f32[64,8,128]{2,1,0:T(8,128)S(1)}, u32[]{:S(2)}, u32[]{:S(2)}) %all-to-all-start.9) | async-done | bytes 262176 | tf_op jit(solution)/shard_map/all_to_all | solution.py:20
  (73 shorter events, 38.6 us)
Async XLA Ops:
  0.6 17.1 %copy-start = (bf16[512,128]{1,0:T(8,128)(2,1)S(1)}, bf16[512,128]{1,0:T(8,128)(2,1)}, u32[]{:S(2)}) copy-start(bf16[512,128]{1,0:T(8,128)(2,1)} %param.9) | copy-start | bytes 393220
  2.6 25.8 %all-to-all-start.1 = ((s32[64,1,16]{2,1,0:T(1,128)}), s32[64,1,16]{2,1,0:T(1,128)S(1)}, u32[]{:S(2)}, u32[]{:S(2)}) async-start(s32[64,1,16]{2,1,0:T(1,128)} %bitcast.70), calls=%async_computation.1 | async-start | bytes 65536 | tf_op jit(solution)/shard_map/all_to_all | solution.py:20
  29.7 22.4 %all-to-all-start = ((s32[64,1,64]{2,1,0:T(1,128)}), s32[64,1,64]{2,1,0:T(1,128)S(1)}, u32[]{:S(2)}, u32[]{:S(2)}) async-start(s32[64,1,64]{2,1,0:T(1,128)} %broadcast_in_dim.457), calls=%async_computation | async-start | bytes 65536 | tf_op jit(solution)/shard_map/all_to_all | solution.py:20
  52.1 25.8 %all-to-all-start.2 = ((bf16[64,16,128]{2,1,0:T(8,128)(2,1)}), bf16[64,16,128]{2,1,0:T(8,128)(2,1)S(1)}, u32[]{:S(2)}, u32[]{:S(2)}) async-start(bf16[64,16,128]{2,1,0:T(8,128)(2,1)} %bitcast.71), calls=%async_computation.2 | async-start | bytes 524288 | tf_op jit(solution)/shard_map/all_to_all | solution.py:20
  79.1 23.9 %all-to-all-start.3 = ((bf16[64,8,128]{2,1,0:T(8,128)(2,1)}), bf16[64,8,128]{2,1,0:T(8,128)(2,1)}, u32[]{:S(2)}, u32[]{:S(2)}) async-start(bf16[64,8,128]{2,1,0:T(8,128)(2,1)} %bitcast.73), calls=%async_computation.3 | async-start | bytes 262144 | tf_op jit(solution)/shard_map/all_to_all | solution.py:20
  105.4 24.3 %all-to-all-start.4 = ((bf16[64,48,128]{2,1,0:T(8,128)(2,1)}), bf16[64,48,128]{2,1,0:T(8,128)(2,1)S(1)}, u32[]{:S(2)}, u32[]{:S(2)}) async-start(bf16[64,48,128]{2,1,0:T(8,128)(2,1)} %reshape.452), calls=%async_computation.4 | async-start | bytes 1572864 | tf_op jit(solution)/shard_map/all_to_all | solution.py:20
  129.8 16.1 %copy-start.2 = (bf16[512,512]{1,0:T(8,128)(2,1)S(1)}, bf16[512,512]{1,0:T(8,128)(2,1)}, u32[]{:S(2)}) copy-start(bf16[512,512]{1,0:T(8,128)(2,1)} %all_gather.7) | copy-start | bytes 1572868
  129.8 16.1 %copy-start.4 = (bf16[512,512]{1,0:T(8,128)(2,1)S(1)}, bf16[512,512]{1,0:T(8,128)(2,1)}, u32[]{:S(2)}) copy-start(bf16[512,512]{1,0:T(8,128)(2,1)} %param.17) | copy-start | bytes 1572868
  129.8 16.1 %copy-start.5 = (f32[512]{0:T(512)S(1)}, f32[512]{0:T(512)}, u32[]{:S(2)}) copy-start(f32[512]{0:T(512)} %param.16) | copy-start | bytes 6148
  145.9 25.6 %copy-start.1 = (bf16[128,512]{1,0:T(8,128)(2,1)S(1)}, bf16[128,512]{1,0:T(8,128)(2,1)}, u32[]{:S(2)}) copy-start(bf16[128,512]{1,0:T(8,128)(2,1)} %param.15) | copy-start | bytes 393220
  148.8 17.4 %all-to-all-start.7 = ((f32[64,1,512]{2,1,0:T(1,128)}), f32[64,1,512]{2,1,0:T(1,128)S(1)}, u32[]{:S(2)}, u32[]{:S(2)}) async-start(f32[64,1,512]{2,1,0:T(1,128)} %broadcast_in_dim.574), calls=%async_computation.7 | async-start | bytes 262144 | tf_op jit(solution)/shard_map/all_to_all | solution.py:20
  166.2 0.7 copy-start.3
  166.8 17.2 %all-to-all-start.5 = ((f32[64,2,512]{2,1,0:T(2,128)}), f32[64,2,512]{2,1,0:T(2,128)S(1)}, u32[]{:S(2)}, u32[]{:S(2)}) async-start(f32[64,2,512]{2,1,0:T(2,128)} %reshape.455), calls=%async_computation.5 | async-start | bytes 524288 | tf_op jit(solution)/shard_map/all_to_all | solution.py:20
  184.0 26.7 %all-to-all-start.8 = ((bf16[64,48,128]{2,1,0:T(8,128)(2,1)}), bf16[64,48,128]{2,1,0:T(8,128)(2,1)S(1)}, u32[]{:S(2)}, u32[]{:S(2)}) async-start(bf16[64,48,128]{2,1,0:T(8,128)(2,1)} %bitcast.199), calls=%async_computation.8 | async-start | bytes 1572864 | tf_op jit(solution)/shard_map/all_to_all | solution.py:20
  211.4 21.3 %all-to-all-start.6 = ((f32[64,2,512]{2,1,0:T(2,128)}), f32[64,2,512]{2,1,0:T(2,128)}, u32[]{:S(2)}, u32[]{:S(2)}) async-start(f32[64,2,512]{2,1,0:T(2,128)} %broadcast_in_dim.573), calls=%async_computation.6 | async-start | bytes 524288 | tf_op jit(solution)/shard_map/all_to_all | solution.py:20
  232.7 17.1 %all-to-all-start.9 = ((f32[64,8,128]{2,1,0:T(8,128)}), f32[64,8,128]{2,1,0:T(8,128)S(1)}, u32[]{:S(2)}, u32[]{:S(2)}) async-start(f32[64,8,128]{2,1,0:T(8,128)} %copy.65), calls=%async_computation.9 | async-start | bytes 524288 | tf_op jit(solution)/shard_map/all_to_all | solution.py:20

commit v3 on v1

v3 whole, which is shorter than its diff:
```python
import functools
import math

import jax
import jax.numpy as jnp
from jax import lax
from jax.experimental import pallas as pl
from jax.experimental.pallas import tpu as pltpu
from jax.sharding import PartitionSpec as P

PARTNERS = 6
BF = jnp.bfloat16
F32 = jnp.float32
MESH = pl.DeviceIdType.MESH
LANES = 128
UNIT = 8


def dot(a, b, dims=((1,), (0,))):
    return lax.dot_general(a, b, (dims, ((), ())), preferred_element_type=F32)


def iota(shape, dim):
    return lax.broadcasted_iota(jnp.int32, shape, dim).astype(F32)


def split(x, by):
    whole = jnp.floor((x + 0.5) * (1.0 / by))
    return whole, x - whole * by


def as_rows(ref):
    return ref.reshape(math.prod(ref.shape[:-1]), ref.shape[-1])


def get_rows(ref):
    return as_rows(ref)[...]


def put_rows(ref, value):
    as_rows(ref)[...] = value


def ones_where(condition):
    return jnp.where(condition, 1.0, 0.0).astype(BF)


def kernel(
    blocks,
    members,
    feat,
    target_ref,
    pos,
    tile_hbm,
    w_ref,
    bias_ref,
    og_ref,
    out_ref,
    wg_ref,
    bg_ref,
    fg_ref,
    tv,
    load_s,
    load_r,
    spread_s,
    spread_r,
    pick_t,
    pick,
    serve_s,
    serve_r,
    adj,
    adj_t,
    mixed_r,
    w_all,
    pg,
    outs,
    mg,
    own,
    term_s,
    term_r,
    sum_s,
    sum_r,
    grad_s,
    grad_r,
    total_s,
    total_r,
    find,
    send_sem,
    recv_sem,
    tile_sem,
):
    me = lax.axis_index("blk")
    member = lax.axis_index("rep")
    rows, cols = feat.shape
    slots, tile = tv.shape[1:3]
    tiles = rows // tile
    bucket = 2 * rows // blocks
    wide = w_ref.shape[1]
    unit_rows = bucket + UNIT
    loaded = blocks * unit_rows
    served = blocks * PARTNERS * UNIT
    meets = PARTNERS + 1

    load_tiles = pltpu.make_async_copy(tile_hbm, tv, tile_sem)
    load_tiles.start()
    barrier = pltpu.get_barrier_semaphore()

    def greet(d, _):
        pl.semaphore_signal(
            barrier, inc=1, device_id=(lax.rem(me + d, blocks), member), device_id_type=MESH
        )
        return 0

    lax.fori_loop(1, blocks, greet, 0)
    for d in range(1, members):
        pl.semaphore_signal(
            barrier, inc=1, device_id=(me, lax.rem(member + d, members)), device_id_type=MESH
        )

    def send_all(phase, source, dest):
        def one(d, _):
            peer = lax.rem(me + d, blocks)
            pltpu.make_async_remote_copy(
                src_ref=source(peer),
                dst_ref=dest,
                send_sem=send_sem.at[phase],
                recv_sem=recv_sem.at[phase],
                device_id=(peer, member),
                device_id_type=MESH,
            ).start()
            return 0

        lax.fori_loop(1, blocks, one, 0)

    def send_members(phase, source, dest):
        for d in range(1, members):
            pltpu.make_async_remote_copy(
                src_ref=source,
                dst_ref=dest,
                send_sem=send_sem.at[phase],
                recv_sem=recv_sem.at[phase],
                device_id=(me, lax.rem(member + d, members)),
                device_id_type=MESH,
            ).start()

    def bytes_of(phase, ref):
        return pltpu.make_async_remote_copy(
            src_ref=ref,
            dst_ref=ref,
            send_sem=send_sem.at[phase],
            recv_sem=recv_sem.at[phase],
            device_id=(me, member),
            device_id_type=MESH,
        )

    def others(ref):
        return ref.at[pl.ds(0, ref.shape[0] - 1)]

    def scan(q, state):
        count, found = state
        live = (pos[0, q] >= 0) & (q != me)
        found = tuple(
            jnp.where(live & (count == k), q, f) for k, f in enumerate(found)
        )
        return count + jnp.where(live, 1, 0), found

    zero = jnp.int32(0)
    _, partners = lax.fori_loop(0, blocks, scan, (zero, (zero,) * PARTNERS))

    target = target_ref[...]
    goal, landing = split(target.astype(F32), rows)
    hits = ones_where(goal == iota((blocks, rows), 0))
    before = ones_where(iota((rows, rows), 0) < iota((rows, rows), 1))
    earlier = dot(hits, before)
    rank = jnp.sum(hits.astype(F32) * earlier, axis=0, keepdims=True)
    high, low = split(landing + 1.0, 16)
    of_rank = ones_where(rank == iota((LANES, rows), 0))
    on_lanes = ((1,), (1,))
    land_high = dot(hits * high.astype(BF), of_rank, on_lanes)
    land_low = dot(hits * low.astype(BF), of_rank, on_lanes)
    lane = lax.broadcasted_iota(jnp.int32, (blocks, LANES), 1)
    listed = jnp.zeros((blocks, LANES), jnp.int32)
    for k in range(PARTNERS):
        listed = jnp.where(lane == k, partners[k], listed)
    notes = jnp.concatenate([land_high, land_low, listed.astype(F32)], axis=0).astype(BF)
    to_unit = ones_where(goal * unit_rows + rank == iota((loaded, rows), 0))
    n_notes = 3 * blocks
    unit, inside = split(iota((loaded, n_notes), 0), unit_rows)
    kind, whose = split(iota((loaded, n_notes), 1), blocks)
    to_note = ones_where((unit == whose) & (inside == kind + bucket))
    filled = dot(to_unit, feat[...]) + dot(to_note, notes)
    put_rows(load_s, filled.astype(BF))

    pl.semaphore_wait(barrier, blocks + members - 2)
    send_all(0, lambda p: load_s.at[p], load_r.at[me])
    send_members(7, w_ref, w_all.at[member])
    load_r[me] = load_s[me]
    w_all[member] = w_ref[...]
    unit, inside = split(iota((n_notes, loaded), 1), unit_rows)
    kind, whose = split(iota((n_notes, loaded), 0), blocks)
    find[...] = ones_where((unit == whose) & (inside == kind + bucket))
    bytes_of(0, others(load_r)).wait_recv()

    got = get_rows(load_r)
    notes = dot(find[...], got)
    unit, inside = split(iota((blocks, loaded), 1), unit_rows)
    fold = ones_where(iota((LANES, loaded), 0) == split(iota((LANES, loaded), 1), unit_rows)[1])
    lands = 16.0 * dot(notes[:blocks].astype(BF), fold) + dot(
        notes[blocks : 2 * blocks].astype(BF), fold
    )
    lands = jnp.where(unit == iota((blocks, loaded), 0), lands, 0.0)
    lands = jnp.sum(lands, axis=0, keepdims=True) - 1.0
    regroup = ones_where(lands == iota((rows, loaded), 0))
    regrouped = dot(regroup, got).astype(BF)
    put_rows(spread_s, regrouped)
    send_all(1, lambda p: spread_s.at[p], spread_r.at[me])
    spread_r[me] = spread_s[me]

    lists = notes[2 * blocks :].astype(BF)
    chunk = rows

    def fill_pick_t(i, _):
        at = iota((chunk, blocks), 0) + (i * chunk).astype(F32)
        for_whom = ones_where(split(at, PARTNERS * UNIT)[0] == iota((chunk, blocks), 1))
        lane_at = iota((chunk, LANES), 0) + (i * chunk).astype(F32)
        nth, row = split(lane_at, UNIT)
        nth = split(nth, PARTNERS)[1]
        listed = jnp.where(nth == iota((chunk, LANES), 1), dot(for_whom, lists), 0.0)
        wanted = dot(listed.astype(BF), jnp.ones((LANES, rows), BF))
        row = iota((chunk, rows), 0) + (i * chunk).astype(F32)
        row = split(row, UNIT)[1]
        match = ones_where(wanted * UNIT + row == iota((chunk, rows), 1))
        pick_t[pl.ds(pl.multiple_of(i * chunk, chunk), chunk), :] = match
        return 0

    lax.fori_loop(0, served // chunk, fill_pick_t, 0)
    bytes_of(1, others(spread_r)).wait_recv()
    serving = dot(pick_t[...], get_rows(spread_r)).astype(BF)
    put_rows(serve_s, serving)
    send_all(2, lambda p: serve_s.at[p], serve_r.at[:, me])
    serve_r[:, me] = serve_s[me]

    load_tiles.wait()
    for k in range(meets):
        q = me if k == PARTNERS else partners[k]
        places = [pos[s, q] for s in range(slots)]
        for i in range(tiles):
            for j in range(tiles):
                chosen = zero
                live = zero
                for s in range(slots):
                    match = places[s] == i * tiles + j
                    chosen = jnp.where(match, s, chosen)
                    live = jnp.where(match, 1, live)
                values = tv[q, chosen]
                values = values * jnp.full(values.shape, live, jnp.int32).astype(F32).astype(BF)
                adj[pl.ds(i * tile, tile), pl.ds(k * rows + j * tile, tile)] = values
                adj_t[pl.ds(k * rows + j * tile, tile), pl.ds(i * tile, tile)] = values.T

    nth, row = split(iota((LANES, served), 1), UNIT)
    nth = split(nth, PARTNERS)[1]
    listed = dot(lists, ones_where(nth == iota((LANES, served), 0)))
    for_whom, row = split(iota((blocks, served), 1), PARTNERS * UNIT)
    listed = jnp.where(for_whom == iota((blocks, served), 0), listed, 0.0)
    wanted = jnp.sum(listed, axis=0, keepdims=True)
    wanted = wanted * UNIT + split(iota((1, served), 1), UNIT)[1]
    pick[...] = ones_where(wanted == iota((rows, served), 0))

    bytes_of(2, others(serve_s)).wait_recv()
    away = PARTNERS * rows
    mixed = dot(adj[:, :away], get_rows(serve_r))
    mixed = (mixed + dot(adj[:, away:], regrouped)).astype(BF)
    mixed_r[member] = mixed
    send_members(8, mixed_r.at[member], mixed_r.at[member])
    bytes_of(7, others(w_all)).wait_recv()
    bytes_of(8, others(mixed_r)).wait_recv()

    share = rows // members
    bias_part = jnp.zeros((1, wide), F32)
    for c in range(members):
        part = pl.ds(c * share, share)
        pre = dot(mixed_r[0, part], w_all[0])
        for r in range(1, members):
            pre = pre + dot(mixed_r[r, part], w_all[r])
        pre = pre + bias_ref[...]
        sigma = jax.nn.sigmoid(pre)
        outs[c] = (pre * sigma).astype(BF)
        grad = og_ref[part, :].astype(F32) * sigma * (1.0 + pre * (1.0 - sigma))
        grad = grad.astype(BF)
        pg[part, :] = grad
        bias_part = bias_part + jnp.sum(grad.astype(F32), axis=0, keepdims=True)
        mg[part, :] = dot(grad, w_ref[...], on_lanes).astype(BF)
    out_ref[...] = outs[member]

    put_rows(term_s, dot(adj_t[:away], mg[...]).astype(BF))
    send_all(3, lambda p: term_s.at[:, p], term_r.at[me])
    term_r[me] = term_s[:, me]
    own[...] = dot(adj_t[away:], mg[...])

    weight_part = dot(mixed.T, pg[...])
    groups = wide // LANES
    per_peer = (cols // UNIT) * groups // blocks
    bands = UNIT // groups
    for p in range(blocks):
        for t in range(per_peer):
            band, group = divmod(p * per_peer + t, groups)
            for b in range(bands):
                top = band * UNIT + b * groups
                grad_s[p, t * bands + b] = weight_part[
                    top : top + groups, group * LANES : (group + 1) * LANES
                ]
        for g in range(groups):
            grad_s[p, per_peer * bands, g : g + 1, :] = bias_part[
                :, g * LANES : (g + 1) * LANES
            ]
    send_all(5, lambda p: grad_s.at[p], grad_r.at[me])
    grad_r[me] = grad_s[me]

    bytes_of(3, others(term_r)).wait_recv()
    sums = dot(pick[...], get_rows(term_r))
    put_rows(sum_s, sums.astype(BF))
    send_all(4, lambda p: sum_s.at[p], sum_r.at[me])
    sum_r[me] = sum_s[me]

    bytes_of(5, others(grad_r)).wait_recv()
    total = jnp.sum(grad_r[...], axis=0)
    total_s[...] = total[: per_peer * bands]
    bg_ref[...] = total[per_peer * bands]
    send_all(6, lambda p: total_s, total_r.at[me])
    total_r[me] = total_s[...]

    bytes_of(4, others(sum_r)).wait_recv()
    back = get_rows(sum_r).astype(F32)
    fg_ref[...] = (back + own[...]).astype(BF)

    bytes_of(6, others(total_r)).wait_recv()
    for p in range(blocks):
        for t in range(per_peer):
            band, group = divmod(p * per_peer + t, groups)
            for b in range(bands):
                top = band * UNIT + b * groups
                wg_ref[top : top + groups, group * LANES : (group + 1) * LANES] = total_r[
                    p, t * bands + b
                ]

    bytes_of(0, others(load_s)).wait_send()
    bytes_of(1, others(spread_s)).wait_send()
    bytes_of(2, others(serve_s)).wait_send()
    bytes_of(3, others(term_r)).wait_send()
    bytes_of(4, others(sum_s)).wait_send()
    bytes_of(5, others(grad_s)).wait_send()
    bytes_of(6, others(total_r)).wait_send()
    bytes_of(7, others(w_all)).wait_send()
    bytes_of(8, others(mixed_r)).wait_send()


def per_device(
    features,
    row_target,
    tile_values,
    tile_rows,
    tile_cols,
    tile_counts,
    weight,
    layer_bias,
    out_grad,
):
    blocks = lax.axis_size("blk")
    members = lax.axis_size("rep")
    rows, cols = features.shape
    slots, tile = tile_values.shape[2:4]
    tiles = rows // tile
    bucket = 2 * rows // blocks
    assert rows == blocks * UNIT and cols == LANES and bucket % UNIT == 0
    wide = weight.shape[1]
    groups = wide // LANES
    pieces = (cols // UNIT) * groups // blocks * (UNIT // groups)
    units = bucket // UNIT + 1
    meets = PARTNERS + 1
    slot = lax.broadcasted_iota(jnp.int32, (slots, blocks), 0)
    place = tile_rows[0].T * tiles + tile_cols[0].T
    pos = jnp.where(slot < tile_counts, place, -1)

    vmem = pl.BlockSpec(memory_space=pltpu.VMEM)
    output, weight_grad, bias_grad, feature_grad = pl.pallas_call(
        functools.partial(kernel, blocks, members),
        out_shape=(
            jax.ShapeDtypeStruct((rows // members, wide), BF),
            jax.ShapeDtypeStruct((cols, wide), F32),
            jax.ShapeDtypeStruct((groups, LANES), F32),
            jax.ShapeDtypeStruct((rows, cols), BF),
        ),
        in_specs=[
            vmem,
            vmem,
            pl.BlockSpec(memory_space=pltpu.SMEM),
            pl.BlockSpec(memory_space=pl.ANY),
            vmem,
            vmem,
            vmem,
        ],
        out_specs=(vmem,) * 4,
        scratch_shapes=[
            pltpu.VMEM((blocks, slots, tile, tile), BF),
            pltpu.VMEM((blocks, units, UNIT, LANES), BF),
            pltpu.VMEM((blocks, units, UNIT, LANES), BF),
            pltpu.VMEM((blocks, UNIT, LANES), BF),
            pltpu.VMEM((blocks, UNIT, LANES), BF),
            pltpu.VMEM((PARTNERS * rows, rows), BF),
            pltpu.VMEM((rows, PARTNERS * rows), BF),
            pltpu.VMEM((blocks, PARTNERS, UNIT, LANES), BF),
            pltpu.VMEM((PARTNERS, blocks, UNIT, LANES), BF),
            pltpu.VMEM((rows, meets * rows), BF),
            pltpu.VMEM((meets * rows, rows), BF),
            pltpu.VMEM((members, rows, cols), BF),
            pltpu.VMEM((members, cols, wide), BF),
            pltpu.VMEM((rows, wide), BF),
            pltpu.VMEM((members, rows // members, wide), BF),
            pltpu.VMEM((rows, cols), BF),
            pltpu.VMEM((rows, cols), F32),
            pltpu.VMEM((PARTNERS, blocks, UNIT, LANES), BF),
            pltpu.VMEM((blocks, PARTNERS, UNIT, LANES), BF),
            pltpu.VMEM((blocks, UNIT, LANES), BF),
            pltpu.VMEM((blocks, UNIT, LANES), BF),
            pltpu.VMEM((blocks, pieces + 1, groups, LANES), F32),
            pltpu.VMEM((blocks, pieces + 1, groups, LANES), F32),
            pltpu.VMEM((pieces, groups, LANES), F32),
            pltpu.VMEM((blocks, pieces, groups, LANES), F32),
            pltpu.VMEM((3 * blocks, blocks * units * UNIT), BF),
            pltpu.SemaphoreType.DMA((9,)),
            pltpu.SemaphoreType.DMA((9,)),
            pltpu.SemaphoreType.DMA,
        ],
        compiler_params=pltpu.CompilerParams(
            collective_id=0, has_side_effects=True, vmem_limit_bytes=58 * 2**20
        ),
    )(
        features,
        row_target.reshape(1, rows),
        pos,
        tile_values[0],
        weight,
        layer_bias.reshape(1, wide),
        out_grad,
    )
    return output, weight_grad, bias_grad.reshape(wide), feature_grad


def solution(mesh):
    in_specs = (
        P("blk", "rep"),
        P("blk"),
        P("blk", None, None, None, None),
        P("blk", None, None),
        P("blk", None, None),
        P("blk", None),
        P("rep", None),
        P(),
        P("blk", None),
    )
    out_specs = (P(("blk", "rep"), None), P("rep", None), P(), P("blk", "rep"))
    return jax.shard_map(
        per_device, mesh=mesh, in_specs=in_specs, out_specs=out_specs, check_vma=False
    )
```

time: 726 us -> 117 us (0.16)
  the two profiles are of different devices: /device:TPU:32 before, /device:TPU:1 now
where the time goes in v3:
time: 117 us; the launch traced here: 116 us
  Pallas kernels  109 us (93%)
  local copies, waits for them, and re-layouts  6.06 us (5%)
  other arithmetic  1.28 us (1%)
    pallas_call x1, Pallas kernels, per_device(): pl.pallas_call(functools.partial(kernel, blocks, members), out_shape=(jax...  109 us
    unnamed x4, local copies, waits for them, and re-layouts  6.06 us

profile of v3, /device:TPU:1, one launch (start us, length us, event | category | flops | bytes accessed | tf_op | source)
XLA Modules:
  0.0 116.5 jit_solution(13060200010452918134)
XLA Ops:
  0.6 1.3 %bitcast_select_fusion.pos = s32[4,64]{1,0:T(4,128)} fusion(s32[1,64,4]{1,2,0:T(4,128)} %param.13, s32[1,64,4]{1,2,0:T(4,128)} %param.12, s32[64]{0:T(128)} %bitcast.13), kind=kLoop, calls=%fused_computation | loop fusion | flops 1024 | bytes 3328 | tf_op jit(solution)/shard_map/jit(_where)/select_n | solution.py:382
  1.9 108.5 %shard_map.120 = (bf16[128,512]{1,0:T(8,128)(2,1)}, f32[128,512]{1,0:T(8,128)}, f32[4,128]{1,0:T(4,128)}, bf16[512,128]{1,0:T(8,128)(2,1)}) custom-call(bf16[512,128]{1,0:T(8,128)(2,1)} %feat.1, s32[1,512]{1,0:T(1,128)} %bitcast.10, s32[4,64]{1,0:T(4,128)} %bitcast_select_fusion.pos, bf16[64,4,128,128]{3,2,1,0:T(8,128)(2,1)} %bitcast.9, ...), custom_call_target="tpu_custom_call" | custom-call | tf_op jit(solution)/shard_map/pallas_call | solution.py:385
  110.4 1.6 %copy.17 = bf16[128,512]{1,0:T(8,128)(2,1)} copy(bf16[128,512]{1,0:T(8,128)(2,1)} %get-tuple-element.16) | data formatting | bytes 262144
  112.0 1.7 %copy.18 = f32[128,512]{1,0:T(8,128)} copy(f32[128,512]{1,0:T(8,128)} %get-tuple-element.17) | data formatting | bytes 524288
  113.7 1.3 %copy.19 = f32[512]{0:T(512)} copy(f32[512]{0:T(512)} %bitcast.12) | data formatting | bytes 4096
  114.9 1.6 %copy.20 = bf16[512,128]{1,0:T(8,128)(2,1)} copy(bf16[512,128]{1,0:T(8,128)(2,1)} %get-tuple-element.19) | data formatting | bytes 262144

commit v4 on v3

--- a/solution.py
+++ b/solution.py
@@ -14,6 +14,9 @@
 MESH = pl.DeviceIdType.MESH
 LANES = 128
 UNIT = 8
+LINE = 8
+PIECE = 16
+KINDS = 4
 
 
 def dot(a, b, dims=((1,), (0,))):
@@ -39,6 +42,10 @@
 
 def put_rows(ref, value):
     as_rows(ref)[...] = value
+
+
+def step_to(kind, across):
+    return (0, 1, -1, 2 - 4 * (across % 2))[kind]
 
 
 def ones_where(condition):
@@ -85,6 +92,8 @@
     total_s,
     total_r,
     find,
+    offset,
+    bias_s,
     send_sem,
     recv_sem,
     tile_sem,
@@ -98,7 +107,14 @@
     wide = w_ref.shape[1]
     unit_rows = bucket + UNIT
     loaded = blocks * unit_rows
-    served = blocks * PARTNERS * UNIT
+    lines = blocks // LINE
+    across = lax.div(me, LINE)
+    along = lax.rem(me, LINE)
+    half = LINE // 2
+    my_class = across * half + lax.rem(along, half)
+    near = lines * KINDS
+    served = near * PARTNERS * PIECE
+    held = blocks * PIECE
     meets = PARTNERS + 1
 
     load_tiles = pltpu.make_async_copy(tile_hbm, tv, tile_sem)
@@ -131,6 +147,46 @@
             return 0
 
         lax.fori_loop(1, blocks, one, 0)
+
+    def whom(index):
+        turn, kind = split(index, KINDS)
+        to = turn + across.astype(F32)
+        to = jnp.where(to >= lines, to - lines, to)
+        far = 2.0 - 4.0 * split(to, 2)[1]
+        step = jnp.where(kind == 1, 1.0, jnp.where(kind == 2, -1.0, far))
+        at = jnp.where(kind == 0, 0.0, step) + along.astype(F32)
+        at = jnp.where(at < 0, at + LINE, at)
+        at = jnp.where(at >= LINE, at - LINE, at)
+        return to * LINE + at
+
+    def send_near(phase, make):
+        for kind in range(KINDS):
+
+            def one(turn, _, kind=kind):
+                peer, source, dest = make(turn, kind)
+                pltpu.make_async_remote_copy(
+                    src_ref=source,
+                    dst_ref=dest,
+                    send_sem=send_sem.at[phase],
+                    recv_sem=recv_sem.at[phase],
+                    device_id=(peer, member),
+                    device_id_type=MESH,
+                ).start()
+                return 0
+
+            lax.fori_loop(1 if kind == 0 else 0, lines, one, 0)
+
+    def serve(turn, kind):
+        to = lax.rem(across + turn, lines)
+        at = lax.rem(along + step_to(kind, to) + LINE, LINE)
+        return to * LINE + at, serve_s.at[turn * KINDS + kind], serve_r.at[:, my_class]
+
+    def give_back(turn, kind):
+        to = lax.rem(across + turn, lines)
+        at = lax.rem(along - step_to(kind, across) + LINE, LINE)
+        place = lax.rem(lines - turn, lines) * KINDS + kind
+        held_class = to * half + lax.rem(at, half)
+        return to * LINE + at, term_s.at[:, held_class], term_r.at[place]
 
     def send_members(phase, source, dest):
         for d in range(1, members):
@@ -199,6 +255,8 @@
     unit, inside = split(iota((n_notes, loaded), 1), unit_rows)
     kind, whose = split(iota((n_notes, loaded), 0), blocks)
     find[...] = ones_where((unit == whose) & (inside == kind + bucket))
+    shift = split(iota(offset.shape, 0), PIECE)[1]
+    offset[...] = iota(offset.shape, 1) - shift
     bytes_of(0, others(load_r)).wait_recv()
 
     got = get_rows(load_r)
@@ -213,32 +271,33 @@
     regroup = ones_where(lands == iota((rows, loaded), 0))
     regrouped = dot(regroup, got).astype(BF)
     put_rows(spread_s, regrouped)
-    send_all(1, lambda p: spread_s.at[p], spread_r.at[me])
-    spread_r[me] = spread_s[me]
+
+    def class_of(peer):
+        return lax.div(peer, LINE) * half + lax.rem(lax.rem(peer, LINE), half)
+
+    send_all(1, lambda p: spread_s.at[class_of(p)], spread_r.at[me])
+    spread_r[me] = spread_s[my_class]
 
     lists = notes[2 * blocks :].astype(BF)
     chunk = rows
 
     def fill_pick_t(i, _):
-        at = iota((chunk, blocks), 0) + (i * chunk).astype(F32)
-        for_whom = ones_where(split(at, PARTNERS * UNIT)[0] == iota((chunk, blocks), 1))
-        lane_at = iota((chunk, LANES), 0) + (i * chunk).astype(F32)
-        nth, row = split(lane_at, UNIT)
+        first = (i * chunk).astype(F32)
+        place = split(iota((chunk, blocks), 0) + first, PARTNERS * PIECE)[0]
+        for_whom = ones_where(whom(place) == iota((chunk, blocks), 1))
+        nth = split(iota((chunk, LANES), 0) + first, PIECE)[0]
         nth = split(nth, PARTNERS)[1]
         listed = jnp.where(nth == iota((chunk, LANES), 1), dot(for_whom, lists), 0.0)
-        wanted = dot(listed.astype(BF), jnp.ones((LANES, rows), BF))
-        row = iota((chunk, rows), 0) + (i * chunk).astype(F32)
-        row = split(row, UNIT)[1]
-        match = ones_where(wanted * UNIT + row == iota((chunk, rows), 1))
+        wanted = dot(listed.astype(BF), jnp.full((LANES, held), PIECE, BF))
+        match = ones_where(wanted == offset[...])
         pick_t[pl.ds(pl.multiple_of(i * chunk, chunk), chunk), :] = match
         return 0
 
     lax.fori_loop(0, served // chunk, fill_pick_t, 0)
     bytes_of(1, others(spread_r)).wait_recv()
-    serving = dot(pick_t[...], get_rows(spread_r)).astype(BF)
-    put_rows(serve_s, serving)
-    send_all(2, lambda p: serve_s.at[p], serve_r.at[:, me])
-    serve_r[:, me] = serve_s[me]
+    put_rows(serve_s, dot(pick_t[...], get_rows(spread_r)).astype(BF))
+    send_near(2, serve)
+    serve_r[:, my_class] = serve_s[0]
 
     load_tiles.wait()
     for k in range(meets):
@@ -257,14 +316,17 @@
                 adj[pl.ds(i * tile, tile), pl.ds(k * rows + j * tile, tile)] = values
                 adj_t[pl.ds(k * rows + j * tile, tile), pl.ds(i * tile, tile)] = values.T
 
-    nth, row = split(iota((LANES, served), 1), UNIT)
+    nth = split(iota((LANES, served), 1), PIECE)[0]
     nth = split(nth, PARTNERS)[1]
     listed = dot(lists, ones_where(nth == iota((LANES, served), 0)))
-    for_whom, row = split(iota((blocks, served), 1), PARTNERS * UNIT)
-    listed = jnp.where(for_whom == iota((blocks, served), 0), listed, 0.0)
+    place = split(iota((1, served), 1), PARTNERS * PIECE)[0]
+    listed = jnp.where(whom(place) == iota((blocks, served), 0), listed, 0.0)
     wanted = jnp.sum(listed, axis=0, keepdims=True)
-    wanted = wanted * UNIT + split(iota((1, served), 1), UNIT)[1]
-    pick[...] = ones_where(wanted == iota((rows, served), 0))
+    wanted = wanted * PIECE + split(iota((1, served), 1), PIECE)[1]
+    part_rows = held // KINDS
+    for c in range(KINDS):
+        at = iota((part_rows, served), 0) + float(c * part_rows)
+        pick[pl.ds(c * part_rows, part_rows), :] = ones_where(wanted == at)
 
     bytes_of(2, others(serve_s)).wait_recv()
     away = PARTNERS * rows
@@ -293,26 +355,27 @@
     out_ref[...] = outs[member]
 
     put_rows(term_s, dot(adj_t[:away], mg[...]).astype(BF))
-    send_all(3, lambda p: term_s.at[:, p], term_r.at[me])
-    term_r[me] = term_s[:, me]
+    send_near(3, give_back)
+    term_r[0] = term_s[:, my_class]
     own[...] = dot(adj_t[away:], mg[...])
 
     weight_part = dot(mixed.T, pg[...])
     groups = wide // LANES
     per_peer = (cols // UNIT) * groups // blocks
-    bands = UNIT // groups
+    bias_s[...] = jnp.zeros(bias_s.shape, F32)
+    for g in range(groups):
+        exact = bias_part[:, g * LANES : (g + 1) * LANES]
+        rounded = exact.astype(BF).astype(F32)
+        bias_s[g : g + 1, :] = rounded
+        bias_s[groups + g : groups + g + 1, :] = exact - rounded
+    bias_rows = bias_s[...].astype(BF)
     for p in range(blocks):
         for t in range(per_peer):
             band, group = divmod(p * per_peer + t, groups)
-            for b in range(bands):
-                top = band * UNIT + b * groups
-                grad_s[p, t * bands + b] = weight_part[
-                    top : top + groups, group * LANES : (group + 1) * LANES
-                ]
-        for g in range(groups):
-            grad_s[p, per_peer * bands, g : g + 1, :] = bias_part[
-                :, g * LANES : (g + 1) * LANES
-            ]
+            grad_s[p, t] = weight_part[
+                band * UNIT : (band + 1) * UNIT, group * LANES : (group + 1) * LANES
+            ].astype(BF)
+        grad_s[p, per_peer] = bias_rows
     send_all(5, lambda p: grad_s.at[p], grad_r.at[me])
     grad_r[me] = grad_s[me]
 
@@ -323,28 +386,33 @@
     sum_r[me] = sum_s[me]
 
     bytes_of(5, others(grad_r)).wait_recv()
-    total = jnp.sum(grad_r[...], axis=0)
-    total_s[...] = total[: per_peer * bands]
-    bg_ref[...] = total[per_peer * bands]
+    total = grad_r[0].astype(F32)
+    for p in range(1, blocks):
+        total = total + grad_r[p].astype(F32)
+    total_s[...] = total[:per_peer].astype(BF)
+    bg_ref[...] = total[per_peer, :groups] + total[per_peer, groups : 2 * groups]
     send_all(6, lambda p: total_s, total_r.at[me])
     total_r[me] = total_s[...]
 
     bytes_of(4, others(sum_r)).wait_recv()
-    back = get_rows(sum_r).astype(F32)
-    fg_ref[...] = (back + own[...]).astype(BF)
+    stretch = half * PIECE
+    for a in range(lines):
+        for side in range(2):
+            for c in range(half):
+                where = pl.ds(a * stretch + c * PIECE, PIECE)
+                own[where, :] += sum_r[a * LINE + side * half + c].astype(F32)
+    fg_ref[...] = own[...].astype(BF)
 
     bytes_of(6, others(total_r)).wait_recv()
     for p in range(blocks):
         for t in range(per_peer):
             band, group = divmod(p * per_peer + t, groups)
-            for b in range(bands):
-                top = band * UNIT + b * groups
-                wg_ref[top : top + groups, group * LANES : (group + 1) * LANES] = total_r[
-                    p, t * bands + b
-                ]
+            wg_ref[
+                band * UNIT : (band + 1) * UNIT, group * LANES : (group + 1) * LANES
+            ] = total_r[p, t].astype(F32)
 
     bytes_of(0, others(load_s)).wait_send()
-    bytes_of(1, others(spread_s)).wait_send()
+    bytes_of(1, others(spread_r)).wait_send()
     bytes_of(2, others(serve_s)).wait_send()
     bytes_of(3, others(term_r)).wait_send()
     bytes_of(4, others(sum_s)).wait_send()
@@ -352,6 +420,11 @@
     bytes_of(6, others(total_r)).wait_send()
     bytes_of(7, others(w_all)).wait_send()
     bytes_of(8, others(mixed_r)).wait_send()
+
+
+def hand_over(*refs):
+    for source, dest in zip(refs[: len(refs) // 2], refs[len(refs) // 2 :]):
+        dest[...] = source[...]
 
 
 def per_device(
@@ -374,7 +447,10 @@
     assert rows == blocks * UNIT and cols == LANES and bucket % UNIT == 0
     wide = weight.shape[1]
     groups = wide // LANES
-    pieces = (cols // UNIT) * groups // blocks * (UNIT // groups)
+    pieces = (cols // UNIT) * groups // blocks
+    half = blocks // 2
+    held = blocks * PIECE
+    away = PARTNERS * rows
     units = bucket // UNIT + 1
     meets = PARTNERS + 1
     slot = lax.broadcasted_iota(jnp.int32, (slots, blocks), 0)
@@ -382,7 +458,7 @@
     pos = jnp.where(slot < tile_counts, place, -1)
 
     vmem = pl.BlockSpec(memory_space=pltpu.VMEM)
-    output, weight_grad, bias_grad, feature_grad = pl.pallas_call(
+    results = pl.pallas_call(
         functools.partial(kernel, blocks, members),
         out_shape=(
             jax.ShapeDtypeStruct((rows // members, wide), BF),
@@ -404,12 +480,12 @@
             pltpu.VMEM((blocks, slots, tile, tile), BF),
             pltpu.VMEM((blocks, units, UNIT, LANES), BF),
             pltpu.VMEM((blocks, units, UNIT, LANES), BF),
-            pltpu.VMEM((blocks, UNIT, LANES), BF),
-            pltpu.VMEM((blocks, UNIT, LANES), BF),
-            pltpu.VMEM((PARTNERS * rows, rows), BF),
-            pltpu.VMEM((rows, PARTNERS * rows), BF),
-            pltpu.VMEM((blocks, PARTNERS, UNIT, LANES), BF),
-            pltpu.VMEM((PARTNERS, blocks, UNIT, LANES), BF),
+            pltpu.VMEM((half, PIECE, LANES), BF),
+            pltpu.VMEM((blocks, PIECE, LANES), BF),
+            pltpu.VMEM((away, held), BF),
+            pltpu.VMEM((held, away), BF),
+            pltpu.VMEM((half, PARTNERS, PIECE, LANES), BF),
+            pltpu.VMEM((PARTNERS, half, PIECE, LANES), BF),
             pltpu.VMEM((rows, meets * rows), BF),
             pltpu.VMEM((meets * rows, rows), BF),
             pltpu.VMEM((members, rows, cols), BF),
@@ -418,15 +494,17 @@
             pltpu.VMEM((members, rows // members, wide), BF),
             pltpu.VMEM((rows, cols), BF),
             pltpu.VMEM((rows, cols), F32),
-            pltpu.VMEM((PARTNERS, blocks, UNIT, LANES), BF),
-            pltpu.VMEM((blocks, PARTNERS, UNIT, LANES), BF),
-            pltpu.VMEM((blocks, UNIT, LANES), BF),
-            pltpu.VMEM((blocks, UNIT, LANES), BF),
-            pltpu.VMEM((blocks, pieces + 1, groups, LANES), F32),
-            pltpu.VMEM((blocks, pieces + 1, groups, LANES), F32),
-            pltpu.VMEM((pieces, groups, LANES), F32),
-            pltpu.VMEM((blocks, pieces, groups, LANES), F32),
+            pltpu.VMEM((PARTNERS, half, PIECE, LANES), BF),
+            pltpu.VMEM((half, PARTNERS, PIECE, LANES), BF),
+            pltpu.VMEM((blocks, PIECE, LANES), BF),
+            pltpu.VMEM((blocks, PIECE, LANES), BF),
+            pltpu.VMEM((blocks, pieces + 1, UNIT, LANES), BF),
+            pltpu.VMEM((blocks, pieces + 1, UNIT, LANES), BF),
+            pltpu.VMEM((pieces, UNIT, LANES), BF),
+            pltpu.VMEM((blocks, pieces, UNIT, LANES), BF),
             pltpu.VMEM((3 * blocks, blocks * units * UNIT), BF),
+            pltpu.VMEM((rows, held), F32),
+            pltpu.VMEM((UNIT, LANES), F32),
             pltpu.SemaphoreType.DMA((9,)),
             pltpu.SemaphoreType.DMA((9,)),
             pltpu.SemaphoreType.DMA,
@@ -443,6 +521,12 @@
         layer_bias.reshape(1, wide),
         out_grad,
     )
+    output, weight_grad, bias_grad, feature_grad = pl.pallas_call(
+        hand_over,
+        out_shape=tuple(jax.ShapeDtypeStruct(r.shape, r.dtype) for r in results),
+        in_specs=[vmem] * len(results),
+        out_specs=(vmem,) * len(results),
+    )(*results)
     return output, weight_grad, bias_grad.reshape(wide), feature_grad
 
 

time: 117 us -> 101 us (0.86)
  Pallas kernels: 109 us -> 98.5 us
  local copies, waits for them, and re-layouts: 6.06 us -> 0 us
    pallas_call x1, Pallas kernels: 109 us -> 96.7 us  [per_device(): pl.pallas_call(functools.partial(kernel, blocks, members), out_shape=(jax...]
    unnamed x4 -> x0, local copies, waits for them, and re-layouts: 6.06 us -> none
    pallas_call x0 -> x1, Pallas kernels: none -> 1.86 us  [per_device(): pl.pallas_call(hand_over, out_shape=tuple((jax.ShapeDtypeStruct(r.shape,...]
where the time goes in v4:
time: 101 us; the launch traced here: 100 us
  Pallas kernels  98.5 us (98%)
  other arithmetic  1.28 us (1%)
    pallas_call x1, Pallas kernels, per_device(): pl.pallas_call(functools.partial(kernel, blocks, members), out_shape=(jax...  96.7 us

profile of v4, /device:TPU:1, one launch (start us, length us, event | category | flops | bytes accessed | tf_op | source)
XLA Modules:
  0.0 100.5 jit_solution(2657758941110472120)
XLA Ops:
  0.6 1.3 %bitcast_select_fusion.pos = s32[4,64]{1,0:T(4,128)} fusion(s32[1,64,4]{1,2,0:T(4,128)} %param.13, s32[1,64,4]{1,2,0:T(4,128)} %param.12, s32[64]{0:T(128)} %bitcast.12), kind=kLoop, calls=%fused_computation | loop fusion | flops 1024 | bytes 3328 | tf_op jit(solution)/shard_map/jit(_where)/select_n | solution.py:458
  1.9 96.7 %shard_map.120 = (bf16[128,512]{1,0:T(8,128)(2,1)}, f32[128,512]{1,0:T(8,128)}, f32[4,128]{1,0:T(4,128)}, bf16[512,128]{1,0:T(8,128)(2,1)}) custom-call(bf16[512,128]{1,0:T(8,128)(2,1)} %feat.1, s32[1,512]{1,0:T(1,128)} %bitcast.10, s32[4,64]{1,0:T(4,128)} %bitcast_select_fusion.pos, bf16[64,4,128,128]{3,2,1,0:T(8,128)(2,1)} %bitcast.9, ...), custom_call_target="tpu_custom_call" | custom-call | tf_op jit(solution)/shard_map/pallas_call | solution.py:461
  98.6 1.9 %shard_map.121 = (bf16[128,512]{1,0:T(8,128)(2,1)}, f32[128,512]{1,0:T(8,128)}, f32[4,128]{1,0:T(4,128)}, bf16[512,128]{1,0:T(8,128)(2,1)}) custom-call(bf16[128,512]{1,0:T(8,128)(2,1)} %get-tuple-element.12.refs_0_, f32[128,512]{1,0:T(8,128)} %get-tuple-element.13.refs_1_, f32[4,128]{1,0:T(4,128)} %get-tuple-element.14.refs_2_, ...), custom_call_target="tpu_custom_call" | custom-call | tf_op jit(solution)/shard_map/pallas_call | solution.py:524

commit v5 on v4

--- a/solution.py
+++ b/solution.py
@@ -42,6 +42,12 @@
 
 def put_rows(ref, value):
     as_rows(ref)[...] = value
+
+
+def put_part(ref, first, count, value):
+    size = math.prod(ref.shape[1:-1])
+    start = pl.multiple_of(first * size, count * size)
+    as_rows(ref)[pl.ds(start, count * size), :] = value
 
 
 def step_to(kind, across):
@@ -159,22 +165,15 @@
         at = jnp.where(at >= LINE, at - LINE, at)
         return to * LINE + at
 
-    def send_near(phase, make):
-        for kind in range(KINDS):
-
-            def one(turn, _, kind=kind):
-                peer, source, dest = make(turn, kind)
-                pltpu.make_async_remote_copy(
-                    src_ref=source,
-                    dst_ref=dest,
-                    send_sem=send_sem.at[phase],
-                    recv_sem=recv_sem.at[phase],
-                    device_id=(peer, member),
-                    device_id_type=MESH,
-                ).start()
-                return 0
-
-            lax.fori_loop(1 if kind == 0 else 0, lines, one, 0)
+    def start(phase, peer, source, dest):
+        pltpu.make_async_remote_copy(
+            src_ref=source,
+            dst_ref=dest,
+            send_sem=send_sem.at[phase],
+            recv_sem=recv_sem.at[phase],
+            device_id=(peer, member),
+            device_id_type=MESH,
+        ).start()
 
     def serve(turn, kind):
         to = lax.rem(across + turn, lines)
@@ -295,8 +294,21 @@
 
     lax.fori_loop(0, served // chunk, fill_pick_t, 0)
     bytes_of(1, others(spread_r)).wait_recv()
-    put_rows(serve_s, dot(pick_t[...], get_rows(spread_r)).astype(BF))
-    send_near(2, serve)
+    turn_rows = KINDS * PARTNERS * PIECE
+
+    def serve_turn(turn, _):
+        part = pl.ds(pl.multiple_of(turn * turn_rows, turn_rows), turn_rows)
+        pieces = dot(pick_t[part, :], get_rows(spread_r)).astype(BF)
+        put_part(serve_s, turn * KINDS, KINDS, pieces)
+        for kind in range(KINDS):
+            start(2, *serve(turn, kind))
+        return 0
+
+    pieces = dot(pick_t[:turn_rows, :], get_rows(spread_r)).astype(BF)
+    put_part(serve_s, 0, KINDS, pieces)
+    for kind in range(1, KINDS):
+        start(2, *serve(0, kind))
+    lax.fori_loop(1, lines, serve_turn, 0)
     serve_r[:, my_class] = serve_s[0]
 
     load_tiles.wait()
@@ -330,17 +342,19 @@
 
     bytes_of(2, others(serve_s)).wait_recv()
     away = PARTNERS * rows
-    mixed = dot(adj[:, :away], get_rows(serve_r))
-    mixed = (mixed + dot(adj[:, away:], regrouped)).astype(BF)
-    mixed_r[member] = mixed
-    send_members(8, mixed_r.at[member], mixed_r.at[member])
+    share = rows // members
+    for c in range(members):
+        part = pl.ds(c * share, share)
+        mixed = dot(adj[part, :away], get_rows(serve_r)) + dot(adj[part, away:], regrouped)
+        mixed_r[member, part] = mixed.astype(BF)
+        send_members(8 + c, mixed_r.at[member, part], mixed_r.at[member, part])
     bytes_of(7, others(w_all)).wait_recv()
-    bytes_of(8, others(mixed_r)).wait_recv()
-
-    share = rows // members
+    some = mixed_r.at[pl.ds(0, members - 1), pl.ds(0, share)]
+
     bias_part = jnp.zeros((1, wide), F32)
     for c in range(members):
         part = pl.ds(c * share, share)
+        bytes_of(8 + c, some).wait_recv()
         pre = dot(mixed_r[0, part], w_all[0])
         for r in range(1, members):
             pre = pre + dot(mixed_r[r, part], w_all[r])
@@ -355,11 +369,19 @@
     out_ref[...] = outs[member]
 
     put_rows(term_s, dot(adj_t[:away], mg[...]).astype(BF))
-    send_near(3, give_back)
+    for kind in range(1, KINDS):
+        start(3, *give_back(0, kind))
+
+    def give_turn(turn, _):
+        for kind in range(KINDS):
+            start(3, *give_back(turn, kind))
+        return 0
+
+    lax.fori_loop(1, lines, give_turn, 0)
     term_r[0] = term_s[:, my_class]
     own[...] = dot(adj_t[away:], mg[...])
 
-    weight_part = dot(mixed.T, pg[...])
+    weight_part = dot(mixed_r[member].T, pg[...])
     groups = wide // LANES
     per_peer = (cols // UNIT) * groups // blocks
     bias_s[...] = jnp.zeros(bias_s.shape, F32)
@@ -380,9 +402,20 @@
     grad_r[me] = grad_s[me]
 
     bytes_of(3, others(term_r)).wait_recv()
-    sums = dot(pick[...], get_rows(term_r))
-    put_rows(sum_s, sums.astype(BF))
-    send_all(4, lambda p: sum_s.at[p], sum_r.at[me])
+    some_lines = max(1, lines // 4)
+    together = some_lines * LINE
+    for turn in range(lines // some_lines):
+        line = lax.rem(lax.div(across, some_lines) * some_lines + turn * some_lines, lines)
+        part = pl.ds(pl.multiple_of(line * LINE * PIECE, together * PIECE), together * PIECE)
+        sums = dot(pick[part, :], get_rows(term_r)).astype(BF)
+        put_part(sum_s, line * LINE, together, sums)
+
+        def hand_back(d, _, line=line):
+            peer = line * LINE + lax.rem(me + d, together)
+            start(4, peer, sum_s.at[peer], sum_r.at[me])
+            return 0
+
+        lax.fori_loop(1 if turn == 0 else 0, together, hand_back, 0)
     sum_r[me] = sum_s[me]
 
     bytes_of(5, others(grad_r)).wait_recv()
@@ -419,7 +452,8 @@
     bytes_of(5, others(grad_s)).wait_send()
     bytes_of(6, others(total_r)).wait_send()
     bytes_of(7, others(w_all)).wait_send()
-    bytes_of(8, others(mixed_r)).wait_send()
+    for c in range(members):
+        bytes_of(8 + c, some).wait_send()
 
 
 def hand_over(*refs):
@@ -505,8 +539,8 @@
             pltpu.VMEM((3 * blocks, blocks * units * UNIT), BF),
             pltpu.VMEM((rows, held), F32),
             pltpu.VMEM((UNIT, LANES), F32),
-            pltpu.SemaphoreType.DMA((9,)),
-            pltpu.SemaphoreType.DMA((9,)),
+            pltpu.SemaphoreType.DMA((8 + members,)),
+            pltpu.SemaphoreType.DMA((8 + members,)),
             pltpu.SemaphoreType.DMA,
         ],
         compiler_params=pltpu.CompilerParams(

time: 101 us -> 95.2 us (0.943)
  Pallas kernels: 98.5 us -> 92.3 us
    pallas_call x1, Pallas kernels: 96.7 us -> 90.5 us  [per_device(): pl.pallas_call(functools.partial(kernel, blocks, members), out_shape=(jax...]
where the time goes in v5:
time: 95.2 us; the launch traced here: 94.2 us
  Pallas kernels  92.3 us (97%)
  other arithmetic  1.28 us (1%)
    pallas_call x1, Pallas kernels, per_device(): pl.pallas_call(functools.partial(kernel, blocks, members), out_shape=(jax...  90.5 us

profile of v5, /device:TPU:1, one launch (start us, length us, event | category | flops | bytes accessed | tf_op | source)
XLA Modules:
  0.0 94.2 jit_solution(17405830059710124066)
XLA Ops:
  0.6 1.3 %bitcast_select_fusion.pos = s32[4,64]{1,0:T(4,128)} fusion(s32[1,64,4]{1,2,0:T(4,128)} %param.13, s32[1,64,4]{1,2,0:T(4,128)} %param.12, s32[64]{0:T(128)} %bitcast.12), kind=kLoop, calls=%fused_computation | loop fusion | flops 1024 | bytes 3328 | tf_op jit(solution)/shard_map/jit(_where)/select_n | solution.py:492
  1.9 90.5 %shard_map.120 = (bf16[128,512]{1,0:T(8,128)(2,1)}, f32[128,512]{1,0:T(8,128)}, f32[4,128]{1,0:T(4,128)}, bf16[512,128]{1,0:T(8,128)(2,1)}) custom-call(bf16[512,128]{1,0:T(8,128)(2,1)} %feat.1, s32[1,512]{1,0:T(1,128)} %bitcast.10, s32[4,64]{1,0:T(4,128)} %bitcast_select_fusion.pos, bf16[64,4,128,128]{3,2,1,0:T(8,128)(2,1)} %bitcast.9, ...), custom_call_target="tpu_custom_call" | custom-call | tf_op jit(solution)/shard_map/pallas_call | solution.py:495
  92.4 1.9 %shard_map.121 = (bf16[128,512]{1,0:T(8,128)(2,1)}, f32[128,512]{1,0:T(8,128)}, f32[4,128]{1,0:T(4,128)}, bf16[512,128]{1,0:T(8,128)(2,1)}) custom-call(bf16[128,512]{1,0:T(8,128)(2,1)} %get-tuple-element.12.refs_0_, f32[128,512]{1,0:T(8,128)} %get-tuple-element.13.refs_1_, f32[4,128]{1,0:T(4,128)} %get-tuple-element.14.refs_2_, ...), custom_call_target="tpu_custom_call" | custom-call | tf_op jit(solution)/shard_map/pallas_call | solution.py:558

commit v6 on v5

--- a/solution.py
+++ b/solution.py
@@ -15,6 +15,7 @@
 LANES = 128
 UNIT = 8
 LINE = 8
+LIST_AT = 64
 PIECE = 16
 KINDS = 4
 
@@ -97,9 +98,14 @@
     grad_r,
     total_s,
     total_r,
-    find,
     offset,
+    note_s,
+    note_r,
+    flat,
     bias_s,
+    line_r,
+    line_s,
+    plane_r,
     send_sem,
     recv_sem,
     tile_sem,
@@ -111,8 +117,8 @@
     tiles = rows // tile
     bucket = 2 * rows // blocks
     wide = w_ref.shape[1]
-    unit_rows = bucket + UNIT
-    loaded = blocks * unit_rows
+    loaded = blocks * bucket
+    to_notes = 8 + members
     lines = blocks // LINE
     across = lax.div(me, LINE)
     along = lax.rem(me, LINE)
@@ -236,38 +242,36 @@
     lane = lax.broadcasted_iota(jnp.int32, (blocks, LANES), 1)
     listed = jnp.zeros((blocks, LANES), jnp.int32)
     for k in range(PARTNERS):
-        listed = jnp.where(lane == k, partners[k], listed)
-    notes = jnp.concatenate([land_high, land_low, listed.astype(F32)], axis=0).astype(BF)
-    to_unit = ones_where(goal * unit_rows + rank == iota((loaded, rows), 0))
-    n_notes = 3 * blocks
-    unit, inside = split(iota((loaded, n_notes), 0), unit_rows)
-    kind, whose = split(iota((loaded, n_notes), 1), blocks)
-    to_note = ones_where((unit == whose) & (inside == kind + bucket))
-    filled = dot(to_unit, feat[...]) + dot(to_note, notes)
-    put_rows(load_s, filled.astype(BF))
+        listed = jnp.where(lane == LIST_AT + k, partners[k], listed)
+    notes = 16.0 * land_high + land_low + listed.astype(F32)
+    for p in range(blocks):
+        note_s[p] = notes[p : p + 1, :]
+    to_slot = ones_where(goal * bucket + rank == iota((loaded, rows), 0))
+    put_rows(load_s, dot(to_slot, feat[...]).astype(BF))
 
     pl.semaphore_wait(barrier, blocks + members - 2)
+    send_all(to_notes, lambda p: note_s.at[p], note_r.at[me])
     send_all(0, lambda p: load_s.at[p], load_r.at[me])
+    note_r[me] = note_s[me]
     send_members(7, w_ref, w_all.at[member])
     load_r[me] = load_s[me]
     w_all[member] = w_ref[...]
-    unit, inside = split(iota((n_notes, loaded), 1), unit_rows)
-    kind, whose = split(iota((n_notes, loaded), 0), blocks)
-    find[...] = ones_where((unit == whose) & (inside == kind + bucket))
     shift = split(iota(offset.shape, 0), PIECE)[1]
     offset[...] = iota(offset.shape, 1) - shift
-    bytes_of(0, others(load_r)).wait_recv()
-
-    got = get_rows(load_r)
-    notes = dot(find[...], got)
-    unit, inside = split(iota((blocks, loaded), 1), unit_rows)
-    fold = ones_where(iota((LANES, loaded), 0) == split(iota((LANES, loaded), 1), unit_rows)[1])
-    lands = 16.0 * dot(notes[:blocks].astype(BF), fold) + dot(
-        notes[blocks : 2 * blocks].astype(BF), fold
-    )
+    fold = ones_where(iota((LANES, loaded), 0) == split(iota((LANES, loaded), 1), bucket)[1])
+    bytes_of(to_notes, others(note_r)).wait_recv()
+    for p in range(blocks):
+        flat[p : p + 1, :] = note_r[p]
+    notes = flat[...]
+    high, low = split(notes, 16)
+    lands = 16.0 * dot(high.astype(BF), fold) + dot(low.astype(BF), fold)
+    unit = split(iota((blocks, loaded), 1), bucket)[0]
     lands = jnp.where(unit == iota((blocks, loaded), 0), lands, 0.0)
     lands = jnp.sum(lands, axis=0, keepdims=True) - 1.0
     regroup = ones_where(lands == iota((rows, loaded), 0))
+
+    bytes_of(0, others(load_r)).wait_recv()
+    got = get_rows(load_r)
     regrouped = dot(regroup, got).astype(BF)
     put_rows(spread_s, regrouped)
 
@@ -277,7 +281,7 @@
     send_all(1, lambda p: spread_s.at[class_of(p)], spread_r.at[me])
     spread_r[me] = spread_s[my_class]
 
-    lists = notes[2 * blocks :].astype(BF)
+    lists = notes.astype(BF)
     chunk = rows
 
     def fill_pick_t(i, _):
@@ -285,7 +289,7 @@
         place = split(iota((chunk, blocks), 0) + first, PARTNERS * PIECE)[0]
         for_whom = ones_where(whom(place) == iota((chunk, blocks), 1))
         nth = split(iota((chunk, LANES), 0) + first, PIECE)[0]
-        nth = split(nth, PARTNERS)[1]
+        nth = split(nth, PARTNERS)[1] + LIST_AT
         listed = jnp.where(nth == iota((chunk, LANES), 1), dot(for_whom, lists), 0.0)
         wanted = dot(listed.astype(BF), jnp.full((LANES, held), PIECE, BF))
         match = ones_where(wanted == offset[...])
@@ -329,7 +333,7 @@
                 adj_t[pl.ds(k * rows + j * tile, tile), pl.ds(i * tile, tile)] = values.T
 
     nth = split(iota((LANES, served), 1), PIECE)[0]
-    nth = split(nth, PARTNERS)[1]
+    nth = split(nth, PARTNERS)[1] + LIST_AT
     listed = dot(lists, ones_where(nth == iota((LANES, served), 0)))
     place = split(iota((1, served), 1), PARTNERS * PIECE)[0]
     listed = jnp.where(whom(place) == iota((blocks, served), 0), listed, 0.0)
@@ -381,25 +385,35 @@
     term_r[0] = term_s[:, my_class]
     own[...] = dot(adj_t[away:], mg[...])
 
+    groups = wide // LANES
+    for g in range(groups):
+        bias_s[g : g + 1, :] = bias_part[:, g * LANES : (g + 1) * LANES]
+    for d in range(1, LINE):
+        peer = across * LINE + lax.rem(along + d, LINE)
+        start(to_notes + 1, peer, bias_s, line_r.at[along])
+    line_r[along] = bias_s[...]
+
     weight_part = dot(mixed_r[member].T, pg[...])
-    groups = wide // LANES
     per_peer = (cols // UNIT) * groups // blocks
-    bias_s[...] = jnp.zeros(bias_s.shape, F32)
-    for g in range(groups):
-        exact = bias_part[:, g * LANES : (g + 1) * LANES]
-        rounded = exact.astype(BF).astype(F32)
-        bias_s[g : g + 1, :] = rounded
-        bias_s[groups + g : groups + g + 1, :] = exact - rounded
-    bias_rows = bias_s[...].astype(BF)
     for p in range(blocks):
         for t in range(per_peer):
             band, group = divmod(p * per_peer + t, groups)
             grad_s[p, t] = weight_part[
                 band * UNIT : (band + 1) * UNIT, group * LANES : (group + 1) * LANES
             ].astype(BF)
-        grad_s[p, per_peer] = bias_rows
     send_all(5, lambda p: grad_s.at[p], grad_r.at[me])
     grad_r[me] = grad_s[me]
+
+    bytes_of(to_notes + 1, others(line_r)).wait_recv()
+    line_s[...] = jnp.sum(line_r[...], axis=0)
+
+    def pass_on(d, _):
+        peer = lax.rem(across + d, lines) * LINE + along
+        start(to_notes + 2, peer, line_s, plane_r.at[across])
+        return 0
+
+    lax.fori_loop(1, lines, pass_on, 0)
+    plane_r[across] = line_s[...]
 
     bytes_of(3, others(term_r)).wait_recv()
     some_lines = max(1, lines // 4)
@@ -422,10 +436,12 @@
     total = grad_r[0].astype(F32)
     for p in range(1, blocks):
         total = total + grad_r[p].astype(F32)
-    total_s[...] = total[:per_peer].astype(BF)
-    bg_ref[...] = total[per_peer, :groups] + total[per_peer, groups : 2 * groups]
+    total_s[...] = total.astype(BF)
     send_all(6, lambda p: total_s, total_r.at[me])
     total_r[me] = total_s[...]
+
+    bytes_of(to_notes + 2, others(plane_r)).wait_recv()
+    bg_ref[...] = jnp.sum(plane_r[...], axis=0)
 
     bytes_of(4, others(sum_r)).wait_recv()
     stretch = half * PIECE
@@ -454,6 +470,9 @@
     bytes_of(7, others(w_all)).wait_send()
     for c in range(members):
         bytes_of(8 + c, some).wait_send()
+    bytes_of(to_notes, others(note_r)).wait_send()
+    bytes_of(to_notes + 1, others(line_r)).wait_send()
+    bytes_of(to_notes + 2, others(plane_r)).wait_send()
 
 
 def hand_over(*refs):
@@ -478,14 +497,13 @@
     slots, tile = tile_values.shape[2:4]
     tiles = rows // tile
     bucket = 2 * rows // blocks
-    assert rows == blocks * UNIT and cols == LANES and bucket % UNIT == 0
+    assert rows == blocks * UNIT and cols == LANES and bucket == PIECE
     wide = weight.shape[1]
     groups = wide // LANES
     pieces = (cols // UNIT) * groups // blocks
     half = blocks // 2
     held = blocks * PIECE
     away = PARTNERS * rows
-    units = bucket // UNIT + 1
     meets = PARTNERS + 1
     slot = lax.broadcasted_iota(jnp.int32, (slots, blocks), 0)
     place = tile_rows[0].T * tiles + tile_cols[0].T
@@ -512,8 +530,8 @@
         out_specs=(vmem,) * 4,
         scratch_shapes=[
             pltpu.VMEM((blocks, slots, tile, tile), BF),
-            pltpu.VMEM((blocks, units, UNIT, LANES), BF),
-            pltpu.VMEM((blocks, units, UNIT, LANES), BF),
+            pltpu.VMEM((blocks, bucket, LANES), BF),
+            pltpu.VMEM((blocks, bucket, LANES), BF),
             pltpu.VMEM((half, PIECE, LANES), BF),
             pltpu.VMEM((blocks, PIECE, LANES), BF),
             pltpu.VMEM((away, held), BF),
@@ -532,15 +550,20 @@
             pltpu.VMEM((half, PARTNERS, PIECE, LANES), BF),
             pltpu.VMEM((blocks, PIECE, LANES), BF),
             pltpu.VMEM((blocks, PIECE, LANES), BF),
-            pltpu.VMEM((blocks, pieces + 1, UNIT, LANES), BF),
-            pltpu.VMEM((blocks, pieces + 1, UNIT, LANES), BF),
+            pltpu.VMEM((blocks, pieces, UNIT, LANES), BF),
+            pltpu.VMEM((blocks, pieces, UNIT, LANES), BF),
             pltpu.VMEM((pieces, UNIT, LANES), BF),
             pltpu.VMEM((blocks, pieces, UNIT, LANES), BF),
-            pltpu.VMEM((3 * blocks, blocks * units * UNIT), BF),
             pltpu.VMEM((rows, held), F32),
-            pltpu.VMEM((UNIT, LANES), F32),
-            pltpu.SemaphoreType.DMA((8 + members,)),
-            pltpu.SemaphoreType.DMA((8 + members,)),
+            pltpu.VMEM((blocks, 1, LANES), F32),
+            pltpu.VMEM((blocks, 1, LANES), F32),
+            pltpu.VMEM((blocks, LANES), F32),
+            pltpu.VMEM((groups, LANES), F32),
+            pltpu.VMEM((LINE, groups, LANES), F32),
+            pltpu.VMEM((groups, LANES), F32),
+            pltpu.VMEM((blocks // LINE, groups, LANES), F32),
+            pltpu.SemaphoreType.DMA((11 + members,)),
+            pltpu.SemaphoreType.DMA((11 + members,)),
             pltpu.SemaphoreType.DMA,
         ],
         compiler_params=pltpu.CompilerParams(

time: 95.2 us -> 93.6 us (0.983)
  no operation moved by 1% of the time
where the time goes in v6:
time: 93.6 us; the launch traced here: 93.4 us
  Pallas kernels  91.5 us (98%)
  other arithmetic  1.28 us (1%)
    pallas_call x1, Pallas kernels, per_device(): pl.pallas_call(functools.partial(kernel, blocks, members), out_shape=(jax...  89.7 us

profile of v6, /device:TPU:1, one launch (start us, length us, event | category | flops | bytes accessed | tf_op | source)
XLA Modules:
  0.0 93.4 jit_solution(3629007125995096654)
XLA Ops:
  0.6 1.3 %bitcast_select_fusion.pos = s32[4,64]{1,0:T(4,128)} fusion(s32[1,64,4]{1,2,0:T(4,128)} %param.13, s32[1,64,4]{1,2,0:T(4,128)} %param.12, s32[64]{0:T(128)} %bitcast.12), kind=kLoop, calls=%fused_computation | loop fusion | flops 1024 | bytes 3328 | tf_op jit(solution)/shard_map/jit(_where)/select_n | solution.py:510
  1.9 89.7 %shard_map.120 = (bf16[128,512]{1,0:T(8,128)(2,1)}, f32[128,512]{1,0:T(8,128)}, f32[4,128]{1,0:T(4,128)}, bf16[512,128]{1,0:T(8,128)(2,1)}) custom-call(bf16[512,128]{1,0:T(8,128)(2,1)} %feat.1, s32[1,512]{1,0:T(1,128)} %bitcast.10, s32[4,64]{1,0:T(4,128)} %bitcast_select_fusion.pos, bf16[64,4,128,128]{3,2,1,0:T(8,128)(2,1)} %bitcast.9, ...), custom_call_target="tpu_custom_call" | custom-call | tf_op jit(solution)/shard_map/pallas_call | solution.py:513
  91.6 1.9 %shard_map.121 = (bf16[128,512]{1,0:T(8,128)(2,1)}, f32[128,512]{1,0:T(8,128)}, f32[4,128]{1,0:T(4,128)}, bf16[512,128]{1,0:T(8,128)(2,1)}) custom-call(bf16[128,512]{1,0:T(8,128)(2,1)} %get-tuple-element.12.refs_0_, f32[128,512]{1,0:T(8,128)} %get-tuple-element.13.refs_1_, f32[4,128]{1,0:T(4,128)} %get-tuple-element.14.refs_2_, ...), custom_call_target="tpu_custom_call" | custom-call | tf_op jit(solution)/shard_map/pallas_call | solution.py:581

commit v7 on v6

--- a/solution.py
+++ b/solution.py
@@ -64,7 +64,9 @@
     members,
     feat,
     target_ref,
-    pos,
+    tile_row,
+    tile_col,
+    counts,
     tile_hbm,
     w_ref,
     bias_ref,
@@ -219,7 +221,7 @@
 
     def scan(q, state):
         count, found = state
-        live = (pos[0, q] >= 0) & (q != me)
+        live = (counts[0, q] > 0) & (q != me)
         found = tuple(
             jnp.where(live & (count == k), q, f) for k, f in enumerate(found)
         )
@@ -318,7 +320,10 @@
     load_tiles.wait()
     for k in range(meets):
         q = me if k == PARTNERS else partners[k]
-        places = [pos[s, q] for s in range(slots)]
+        places = [
+            jnp.where(s < counts[0, q], tile_row[s, q] * tiles + tile_col[s, q], -1)
+            for s in range(slots)
+        ]
         for i in range(tiles):
             for j in range(tiles):
                 chosen = zero
@@ -415,6 +420,14 @@
     lax.fori_loop(1, lines, pass_on, 0)
     plane_r[across] = line_s[...]
 
+    bytes_of(5, others(grad_r)).wait_recv()
+    total = grad_r[0].astype(F32)
+    for p in range(1, blocks):
+        total = total + grad_r[p].astype(F32)
+    total_s[...] = total.astype(BF)
+    send_all(6, lambda p: total_s, total_r.at[me])
+    total_r[me] = total_s[...]
+
     bytes_of(3, others(term_r)).wait_recv()
     some_lines = max(1, lines // 4)
     together = some_lines * LINE
@@ -432,16 +445,16 @@
         lax.fori_loop(1 if turn == 0 else 0, together, hand_back, 0)
     sum_r[me] = sum_s[me]
 
-    bytes_of(5, others(grad_r)).wait_recv()
-    total = grad_r[0].astype(F32)
-    for p in range(1, blocks):
-        total = total + grad_r[p].astype(F32)
-    total_s[...] = total.astype(BF)
-    send_all(6, lambda p: total_s, total_r.at[me])
-    total_r[me] = total_s[...]
-
     bytes_of(to_notes + 2, others(plane_r)).wait_recv()
     bg_ref[...] = jnp.sum(plane_r[...], axis=0)
+
+    bytes_of(6, others(total_r)).wait_recv()
+    for p in range(blocks):
+        for t in range(per_peer):
+            band, group = divmod(p * per_peer + t, groups)
+            wg_ref[
+                band * UNIT : (band + 1) * UNIT, group * LANES : (group + 1) * LANES
+            ] = total_r[p, t].astype(F32)
 
     bytes_of(4, others(sum_r)).wait_recv()
     stretch = half * PIECE
@@ -451,14 +464,6 @@
                 where = pl.ds(a * stretch + c * PIECE, PIECE)
                 own[where, :] += sum_r[a * LINE + side * half + c].astype(F32)
     fg_ref[...] = own[...].astype(BF)
-
-    bytes_of(6, others(total_r)).wait_recv()
-    for p in range(blocks):
-        for t in range(per_peer):
-            band, group = divmod(p * per_peer + t, groups)
-            wg_ref[
-                band * UNIT : (band + 1) * UNIT, group * LANES : (group + 1) * LANES
-            ] = total_r[p, t].astype(F32)
 
     bytes_of(0, others(load_s)).wait_send()
     bytes_of(1, others(spread_r)).wait_send()
@@ -495,7 +500,6 @@
     members = lax.axis_size("rep")
     rows, cols = features.shape
     slots, tile = tile_values.shape[2:4]
-    tiles = rows // tile
     bucket = 2 * rows // blocks
     assert rows == blocks * UNIT and cols == LANES and bucket == PIECE
     wide = weight.shape[1]
@@ -505,10 +509,7 @@
     held = blocks * PIECE
     away = PARTNERS * rows
     meets = PARTNERS + 1
-    slot = lax.broadcasted_iota(jnp.int32, (slots, blocks), 0)
-    place = tile_rows[0].T * tiles + tile_cols[0].T
-    pos = jnp.where(slot < tile_counts, place, -1)
-
+    smem = pl.BlockSpec(memory_space=pltpu.SMEM)
     vmem = pl.BlockSpec(memory_space=pltpu.VMEM)
     results = pl.pallas_call(
         functools.partial(kernel, blocks, members),
@@ -521,7 +522,9 @@
         in_specs=[
             vmem,
             vmem,
-            pl.BlockSpec(memory_space=pltpu.SMEM),
+            smem,
+            smem,
+            smem,
             pl.BlockSpec(memory_space=pl.ANY),
             vmem,
             vmem,
@@ -572,7 +575,9 @@
     )(
         features,
         row_target.reshape(1, rows),
-        pos,
+        tile_rows[0].T,
+        tile_cols[0].T,
+        tile_counts,
         tile_values[0],
         weight,
         layer_bias.reshape(1, wide),

time: 93.6 us -> 93.7 us (level)
  Pallas kernels: 91.5 us -> 92.8 us
  other arithmetic: 1.28 us -> 0 us
    select_n x1 -> x0, other arithmetic: 1.28 us -> none  [per_device(): pos = jnp.where(slot < tile_counts, place, -1)]
    pallas_call x1, Pallas kernels: 89.7 us -> 90.9 us  [per_device(): pl.pallas_call(functools.partial(kernel, blocks, members), out_shape=(jax...]
where the time goes in v7:
time: 93.7 us; the launch traced here: 93.4 us
  Pallas kernels  92.8 us (99%)
    pallas_call x1, Pallas kernels, per_device(): pl.pallas_call(functools.partial(kernel, blocks, members), out_shape=(jax...  90.9 us

profile of v7, /device:TPU:1, one launch (start us, length us, event | category | flops | bytes accessed | tf_op | source)
XLA Modules:
  0.0 93.4 jit_solution(6792727408772007643)
XLA Ops:
  0.6 90.9 %shard_map.120 = (bf16[128,512]{1,0:T(8,128)(2,1)}, f32[128,512]{1,0:T(8,128)}, f32[4,128]{1,0:T(4,128)}, bf16[512,128]{1,0:T(8,128)(2,1)}) custom-call(bf16[512,128]{1,0:T(8,128)(2,1)} %feat.1, s32[1,512]{1,0:T(1,128)} %bitcast.11, s32[4,64]{1,0:T(4,128)} %bitcast.12, s32[4,64]{1,0:T(4,128)} %bitcast.13, s32[1,64]{1,0:T(1,128)} %counts.1, ...), custom_call_target="tpu_custom_call" | custom-call | tf_op jit(solution)/shard_map/pallas_call | solution.py:514
  91.5 1.9 %shard_map.121 = (bf16[128,512]{1,0:T(8,128)(2,1)}, f32[128,512]{1,0:T(8,128)}, f32[4,128]{1,0:T(4,128)}, bf16[512,128]{1,0:T(8,128)(2,1)}) custom-call(bf16[128,512]{1,0:T(8,128)(2,1)} %get-tuple-element.12.refs_0_, f32[128,512]{1,0:T(8,128)} %get-tuple-element.13.refs_1_, f32[4,128]{1,0:T(4,128)} %get-tuple-element.14.refs_2_, ...), custom_call_target="tpu_custom_call" | custom-call | tf_op jit(solution)/shard_map/pallas_call | solution.py:586

commit v8 on v7

--- a/solution.py
+++ b/solution.py
@@ -420,14 +420,6 @@
     lax.fori_loop(1, lines, pass_on, 0)
     plane_r[across] = line_s[...]
 
-    bytes_of(5, others(grad_r)).wait_recv()
-    total = grad_r[0].astype(F32)
-    for p in range(1, blocks):
-        total = total + grad_r[p].astype(F32)
-    total_s[...] = total.astype(BF)
-    send_all(6, lambda p: total_s, total_r.at[me])
-    total_r[me] = total_s[...]
-
     bytes_of(3, others(term_r)).wait_recv()
     some_lines = max(1, lines // 4)
     together = some_lines * LINE
@@ -447,6 +439,14 @@
 
     bytes_of(to_notes + 2, others(plane_r)).wait_recv()
     bg_ref[...] = jnp.sum(plane_r[...], axis=0)
+
+    bytes_of(5, others(grad_r)).wait_recv()
+    total = grad_r[0].astype(F32)
+    for p in range(1, blocks):
+        total = total + grad_r[p].astype(F32)
+    total_s[...] = total.astype(BF)
+    send_all(6, lambda p: total_s, total_r.at[me])
+    total_r[me] = total_s[...]
 
     bytes_of(6, others(total_r)).wait_recv()
     for p in range(blocks):

time: 93.7 us -> 92.4 us (0.986)
  Pallas kernels: 92.8 us -> 91.6 us
    pallas_call x1, Pallas kernels: 90.9 us -> 89.8 us  [per_device(): pl.pallas_call(functools.partial(kernel, blocks, members), out_shape=(jax...]
where the time goes in v8:
time: 92.4 us; the launch traced here: 92.3 us
  Pallas kernels  91.6 us (99%)
    pallas_call x1, Pallas kernels, per_device(): pl.pallas_call(functools.partial(kernel, blocks, members), out_shape=(jax...  89.8 us
    pallas_call x1, Pallas kernels, per_device(): pl.pallas_call(hand_over, out_shape=tuple((jax.ShapeDtypeStruct(r.shape,...  1.86 us

profile of v8, /device:TPU:1, one launch (start us, length us, event | category | flops | bytes accessed | tf_op | source)
XLA Modules:
  0.0 92.3 jit_solution(8891158065019282340)
XLA Ops:
  0.6 89.8 %shard_map.120 = (bf16[128,512]{1,0:T(8,128)(2,1)}, f32[128,512]{1,0:T(8,128)}, f32[4,128]{1,0:T(4,128)}, bf16[512,128]{1,0:T(8,128)(2,1)}) custom-call(bf16[512,128]{1,0:T(8,128)(2,1)} %feat.1, s32[1,512]{1,0:T(1,128)} %bitcast.11, s32[4,64]{1,0:T(4,128)} %bitcast.12, s32[4,64]{1,0:T(4,128)} %bitcast.13, s32[1,64]{1,0:T(1,128)} %counts.1, ...), custom_call_target="tpu_custom_call" | custom-call | tf_op jit(solution)/shard_map/pallas_call | solution.py:514
  90.4 1.9 %shard_map.121 = (bf16[128,512]{1,0:T(8,128)(2,1)}, f32[128,512]{1,0:T(8,128)}, f32[4,128]{1,0:T(4,128)}, bf16[512,128]{1,0:T(8,128)(2,1)}) custom-call(bf16[128,512]{1,0:T(8,128)(2,1)} %get-tuple-element.12.refs_0_, f32[128,512]{1,0:T(8,128)} %get-tuple-element.13.refs_1_, f32[4,128]{1,0:T(4,128)} %get-tuple-element.14.refs_2_, ...), custom_call_target="tpu_custom_call" | custom-call | tf_op jit(solution)/shard_map/pallas_call | solution.py:586
